TPU v7x, 32 devices: a whole 2x2x4 slice. The times are simulated.
32 devices in a mesh: dp: 4 (over y, x), shard: 8 (over z, core).
Axes of the slice: x: 2, y: 2, z: 4, core: 2. Of those that a mesh axis runs over, the one named last changes fastest.
Arguments:
- inputs: bfloat16 [2, 1024, 8192], P(None, 'dp', 'shard'), may hold values from -6 to 6
- key_panel: bfloat16 [8192, 4096], P('dp', 'shard'), may hold values from -0.0625 to 0.0625
- value_panel: bfloat16 [8192, 4096], P('dp', 'shard'), may hold values from -0.0625 to 0.0625
- short_filters: float32 [2, 4096, 7], P(None, 'shard'), may hold values from -2 to 2
- medium_filters: float32 [256, 128], P('shard'), may hold values from -0.5 to 0.5
- lengths: int32 [2], replicated, may hold values from 512 to 1024, as said below
- cotangent: bfloat16 [2, 1024, 4096], P(None, 'dp', 'shard'), may hold values from -0.099609375 to 0.099609375
Outputs:
- mixed: bfloat16 [2, 1024, 4096], P(None, 'dp', 'shard')
- key_grad: bfloat16 [8192, 4096], P('dp', 'shard')
- value_grad: bfloat16 [8192, 4096], P('dp', 'shard')
- short_grad: float32 [2, 4096, 7], P(None, 'shard')
- medium_grad: float32 [256, 128], P('shard')
Inputs may be any that keep to these rules, and one draw needn't show every extreme that they name: `lengths`: each length is a multiple of 16; one window in every draw has the full length 1024, the others are shorter.
All inputs are finite; a program needn't handle non-finite values.
Results may differ from a plain program's by a relative error of at most 0.014.
Values may be sent and summed in bfloat16 or wider, within the bound.
A program may use at most 128 MiB of HBM per device.

v0:
```python
import jax
import jax.numpy as jnp
from jax import lax
from jax.sharding import PartitionSpec as P


def shifted(value, axis, steps):
    count = lax.axis_size(axis)
    first, last = (max(0, -steps), min(count, count - steps))
    return lax.ppermute(value, axis, [(source, source + steps) for source in range(first, last)])


def band(filters, count):
    groups, taps = filters.shape
    width = count + taps - 1
    padded = jnp.concatenate([filters, jnp.zeros((groups, count), jnp.float32)], axis=1)
    tiled = jnp.tile(padded, (1, count))[:, : count * width]
    return tiled.reshape(groups, count, width)


def band_sums(correlation, count, taps):
    groups, _, width = correlation.shape
    flat = correlation.reshape(groups, count * width)
    padded = jnp.concatenate([flat, jnp.zeros((groups, count), jnp.float32)], axis=1)
    skewed = padded.reshape(groups, count, width + 1)
    return jnp.sum(skewed, axis=1)[:, :taps][:, ::-1]


def short_taps(extended, filters, count):
    width = filters.shape[-1]
    total = jnp.zeros(extended.shape[:2] + (count, extended.shape[3]), jnp.float32)
    for tap in range(width):
        begin = width - 1 - tap
        total = total + filters[:, None, None, :, tap] * extended[
            :, :, begin : begin + count
        ].astype(jnp.float32)
    return total


def short_ahead(extended, filters, count):
    width = filters.shape[-1]
    total = jnp.zeros(extended.shape[:2] + (count, extended.shape[3]), jnp.float32)
    for tap in range(width):
        total = total + filters[:, None, None, :, tap] * extended[:, :, tap : tap + count]
    return total


def filter_terms(grads, extended, count, width):
    columns = []
    for tap in range(width):
        begin = width - 1 - tap
        columns.append(
            jnp.sum(grads * extended[:, :, begin : begin + count].astype(jnp.float32), axis=(1, 2))
        )
    return jnp.stack(columns, axis=-1)


def shards(inputs, key_panel, value_panel, short_filters, medium_filters, lengths, cotangent):
    seqs, count, local_width = inputs.shape
    channels = key_panel.shape[1]
    groups, taps = medium_filters.shape
    group_size = channels // groups
    short_width = short_filters.shape[-1]
    span = count + taps - 1
    gathered = (
        lax.all_gather(key_panel, "dp", axis=0, tiled=True),
        lax.all_gather(value_panel, "dp", axis=0, tiled=True),
    )
    panels = jnp.concatenate([gathered[0], gathered[1]], axis=1)
    features = lax.all_gather(inputs, "shard", axis=2, tiled=True)
    projected = jnp.dot(
        features.reshape(seqs * count, -1), panels, preferred_element_type=jnp.float32
    )
    paired = projected.astype(jnp.bfloat16).reshape(seqs, count, 2, channels).transpose(2, 0, 1, 3)
    head_rows = shifted(paired[:, :, count - (short_width - 1) :], "dp", 1)
    extended = jnp.concatenate([head_rows, paired], axis=2)
    smoothed = short_taps(extended, short_filters, count)
    product = (smoothed[0] * smoothed[1]).astype(jnp.bfloat16)
    before = shifted(product[:, count - (taps - 1) :], "dp", 1)
    product_ext = jnp.concatenate([before, product], axis=1).reshape(seqs, span, groups, group_size)
    forward_band = band(medium_filters[:, ::-1], count)
    response = jnp.einsum(
        "gtr,srgm->stgm",
        forward_band,
        product_ext.astype(jnp.float32),
        precision=lax.Precision.HIGHEST,
    ).reshape(seqs, count, channels)
    position = lax.axis_index("dp") * count + jnp.arange(count, dtype=jnp.int32)
    live = (position[None, :] < lengths[:, None])[:, :, None]
    mixed = jnp.where(live, response, 0.0).astype(jnp.bfloat16)
    upstream = jnp.where(live, cotangent, jnp.zeros_like(cotangent))
    after = shifted(upstream[:, : taps - 1], "dp", -1)
    upstream_ext = jnp.concatenate([upstream, after], axis=1).reshape(
        seqs, span, groups, group_size
    )
    backward_band = band(medium_filters, count)
    product_grad = jnp.einsum(
        "gtr,srgm->stgm",
        backward_band,
        upstream_ext.astype(jnp.float32),
        precision=lax.Precision.HIGHEST,
    ).reshape(seqs, count, channels)
    correlation = jnp.einsum(
        "stgm,srgm->gtr",
        upstream.reshape(seqs, count, groups, group_size),
        product_ext,
        preferred_element_type=jnp.float32,
    )
    medium_local = band_sums(correlation, count, taps)
    smooth_grad = jnp.stack([product_grad * smoothed[1], product_grad * smoothed[0]])
    short_local = filter_terms(smooth_grad, extended, count, short_width)
    ahead_rows = shifted(smooth_grad[:, :, : short_width - 1], "dp", -1)
    pair_grad = short_ahead(
        jnp.concatenate([smooth_grad, ahead_rows], axis=2), short_filters, count
    )
    short_grad, medium_grad = lax.psum((short_local, medium_local), "dp")
    outgoing = (
        pair_grad.astype(jnp.bfloat16).transpose(1, 2, 0, 3).reshape(seqs * count, 2 * channels)
    )
    flat_features = features.reshape(seqs * count, -1)
    grads = lax.psum_scatter(
        lax.dot_general(
            flat_features, outgoing, (((0,), (0,)), ((), ())), preferred_element_type=jnp.float32
        ).astype(jnp.bfloat16),
        "dp",
        scatter_dimension=0,
        tiled=True,
    ).astype(jnp.float32)
    key_grad = grads[:, :channels].astype(jnp.bfloat16)
    value_grad = grads[:, channels:].astype(jnp.bfloat16)
    return (mixed, key_grad, value_grad, short_grad, medium_grad)


def solution(mesh):
    return jax.shard_map(
        shards,
        mesh=mesh,
        in_specs=(
            P(None, "dp", "shard"),
            P("dp", "shard"),
            P("dp", "shard"),
            P(None, "shard", None),
            P("shard", None),
            P(),
            P(None, "dp", "shard"),
        ),
        out_specs=(
            P(None, "dp", "shard"),
            P("dp", "shard"),
            P("dp", "shard"),
            P(None, "shard", None),
            P("shard", None),
        ),
        check_vma=False,
    )
```

profile of v0, /device:TPU:0, one launch (start us, length us, event | category | flops | bytes accessed | tf_op | source)
XLA Modules:
  0.0 523.6 jit_solution(11254609745111663512)
XLA Ops:
  11.2 5.3 %tile.20 = f32[32,256,384]{2,1,0:T(8,128)} broadcast(f32[32,384]{1,0:T(8,128)S(1)} %concatenate.29), dimensions={0,2} | broadcast | bytes 12632064 | tf_op jit(solution)/shard_map/tile | solution.py:17
  16.5 17.6 %copy.51 = f32[4,8,256,384]{3,1,2,0:T(8,128)} copy(f32[4,8,256,384]{3,2,1,0:T(8,128)} %bitcast.85) | data formatting | bytes 25165824
  34.1 9.8 %slice.153 = f32[32,98048]{1,0:T(8,128)} slice(f32[32,98304]{1,0:T(8,128)} %bitcast.88), slice={[0:32], [0:98048]} | slice | bytes 25100288 | tf_op jit(solution)/shard_map/slice | solution.py:17
  43.9 18.3 %reshape.111 = f32[32,256,383,1]{2,1,0,3:T(8,128)} reshape(f32[32,98048]{1,0:T(8,128)} %slice.153) | data formatting | bytes 25100288 | tf_op jit(solution)/shard_map/reshape | solution.py:18
  63.2 36.9 %all-gather.4.cloned.1.call-done = bf16[8192,512]{1,0:T(8,128)(2,1)} async-done(((bf16[2048,512]{1,0:T(8,128)(2,1)}), bf16[8192,512]{1,0:T(8,128)(2,1)}) %all-gather.4.cloned.1.call-update) | async-done | bytes 8388624 | tf_op jit(solution)/shard_map/all_gather | solution.py:66
  100.2 89.5 %all-gather.6.cloned.1.call-done = bf16[8192,512]{1,0:T(8,128)(2,1)} async-done(((bf16[2048,512]{1,0:T(8,128)(2,1)}), bf16[8192,512]{1,0:T(8,128)(2,1)}) %all-gather.6.cloned.1.call-update) | async-done | bytes 8388624 | tf_op jit(solution)/shard_map/all_gather | solution.py:67
  189.7 83.7 %all-gather.8.cloned.1.call-done = bf16[2,256,8192]{2,1,0:T(8,128)(2,1)} async-done(((bf16[2,256,1024]{2,1,0:T(8,128)(2,1)}), bf16[2,256,8192]{2,1,0:T(8,128)(2,1)}) %all-gather.8.cloned.1.call-update) | async-done | bytes 8388624 | tf_op jit(solution)/shard_map/all_gather | solution.py:70
  273.4 13.9 %fusion.37 = bf16[512,1024]{0,1:T(8,128)(2,1)S(1)} fusion(bf16[512,8192]{1,0:T(8,128)(2,1)} %bitcast.99, bf16[8192,512]{1,0:T(8,128)(2,1)} %all-gather.6.cloned.1.call-done, bf16[8192,512]{1,0:T(8,128)(2,1)} %all-gather.4.cloned.1.call-done), kind=kOutput, calls=%fused_computation.68 | convolution fusion | flops 8624013312 | bytes 26214400 | tf_op jit(solution)/shard_map/dot_general | solution.py:71
  288.0 3.5 collective-permute-start
  291.6 9.7 %fusion.34 = f32[2,256,32,16]{1,3,0,2:T(8,128)S(1)} fusion(f32[32,256,383,1]{2,1,0,3:T(8,128)} %reshape.111, bf16[2,383,32,16]{1,3,2,0:T(8,128)(2,1)S(1)} %bitcast.97), kind=kOutput, calls=%fused_computation.67 | convolution fusion | flops 1204813824 | bytes 14383104 | tf_op jit(solution)/shard_map/gtr,srgm->stgm/dot_general | solution.py:97
  303.1 3.8 fusion.13
  311.9 5.2 collective-permute-done.3
  319.8 5.3 %fusion.47 = bf16[2,256,2,512]{1,3,0,2:T(8,128)(2,1)} fusion(f32[2,2,262,512]{2,3,1,0:T(8,128)S(1)} %pad_maximum_fusion, f32[2,512]{1,0:T(2,128)S(1)} %get-tuple-element.49, f32[2,512]{1,0:T(2,128)S(1)} %get-tuple-element.50, f32[2,512]{1,0:T(2,128)S(1)} %get-tuple-element.45, f32[2,512]{1,0:T(2,128)S(1)} %get-tuple-element.46, ...), kind=kLoop, calls=%fused_computation.82 | loop fusion | flops 7864320 | bytes 15757312 | tf_op jit(solution)/shard_map/transpose | solution.py:118
  325.1 3.7 copy.44
  330.2 15.9 %convert_bitcast_fusion = bf16[8192,1024]{0,1:T(8,128)(2,1)} fusion(bf16[512,1024]{1,0:T(8,128)(2,1)S(1)} %bitcast.98, bf16[512,8192]{1,0:T(8,128)(2,1)} %bitcast.100), kind=kOutput, calls=%fused_computation.4 | convolution fusion | flops 8598323200 | bytes 26214400 | tf_op jit(solution)/shard_map/dot_general | solution.py:122
  346.2 5.3 %tile.8 = f32[32,256,384]{2,1,0:T(8,128)} broadcast(f32[32,384]{1,0:T(8,128)S(1)} %concatenate.27), dimensions={0,2} | broadcast | bytes 12632064 | tf_op jit(solution)/shard_map/tile | solution.py:17
  351.5 16.8 %copy.50 = f32[4,8,256,384]{3,1,2,0:T(8,128)} copy(f32[4,8,256,384]{3,2,1,0:T(8,128)} %bitcast.86) | data formatting | bytes 25165824
  368.3 10.6 %slice.151 = f32[32,98048]{1,0:T(8,128)} slice(f32[32,98304]{1,0:T(8,128)} %bitcast.89), slice={[0:32], [0:98048]} | slice | bytes 25100288 | tf_op jit(solution)/shard_map/slice | solution.py:17
  378.9 18.3 %reshape.110 = f32[32,256,383,1]{2,1,0,3:T(8,128)} reshape(f32[32,98048]{1,0:T(8,128)} %slice.151) | data formatting | bytes 25100288 | tf_op jit(solution)/shard_map/reshape | solution.py:18
  398.4 4.8 collective-permute-start.1
  403.2 6.3 %fusion.19 = (f32[2,512]{1,0:T(2,128)S(1)}, f32[2,512]{1,0:T(2,128)S(1)}, f32[2,512]{1,0:T(2,128)S(1)}, f32[2,512]{1,0:T(2,128)S(1)}, f32[2,512]{1,0:T(2,128)S(1...) fusion(bf16[2,2,256,512]{2,3,1,0:T(8,128)(2,1)S(1)} %bitcast.92, bf16[2,2,6,512]{2,3,1,0:T(8,128)(2,1)} %copy-done.5, ...), kind=kLoop, calls=%fused_computation.45 | loop fusion | flops 20964352 | bytes 4247552 | tf_op jit(solution)/shard_map/reduce_sum | solution.py:53
  409.6 5.2 collective-permute-done.1
  415.1 6.3 %convolution_bitcast_fusion = f32[32,256,383]{2,1,0:T(8,128)} fusion(bf16[2,256,32,16]{1,3,2,0:T(8,128)(2,1)S(1)} %bitcast.95, bf16[2,383,32,16]{1,3,2,0:T(8,128)(2,1)S(1)} %bitcast.93), kind=kOutput, calls=%fused_computation.10 | convolution fusion | flops 200802304 | bytes 13858816 | tf_op jit(solution)/shard_map/stgm,srgm->gtr/dot_general | solution.py:103
  421.4 13.3 %reshape.108 = f32[32,98048]{1,0:T(8,128)} reshape(f32[32,256,383]{2,1,0:T(8,128)} %convolution_bitcast_fusion) | data formatting | bytes 25100288 | tf_op jit(solution)/shard_map/reshape | solution.py:23
  434.7 10.1 %concatenate.31 = f32[32,98304]{1,0:T(8,128)} pad(f32[32,98048]{1,0:T(8,128)} %reshape.108, f32[]{:T(128)} %constant.2.clone.1), padding=0_0x0_256 | pad | bytes 25133060 | tf_op jit(solution)/shard_map/concatenate | solution.py:24
  444.8 11.8 %copy.53 = f32[4,8,256,384]{3,2,1,0:T(8,128)} copy(f32[4,8,256,384]{3,1,2,0:T(8,128)} %bitcast.87) | data formatting | bytes 25165824
  456.6 5.3 %bitcast_reduce_fusion = f32[32,384]{1,0:T(8,128)S(1)} fusion(f32[4,8,256,384]{3,2,1,0:T(8,128)} %copy.53), kind=kLoop, calls=%fused_computation.5 | loop fusion | flops 3133440 | bytes 12632064 | tf_op jit(solution)/shard_map/reduce_sum | solution.py:26
  462.0 11.4 %fusion.31 = bf16[2,256,32,16]{1,3,0,2:T(8,128)(2,1)S(1)} fusion(f32[32,256,383,1]{2,1,0,3:T(8,128)} %reshape.110, bf16[2,383,32,16]{1,3,2,0:T(8,128)(2,1)S(1)} %bitcast.94), kind=kOutput, calls=%fused_computation.66 | convolution fusion | flops 1204813824 | bytes 13858816 | tf_op jit(solution)/shard_map/gtr,srgm->stgm/dot_general | solution.py:82
  474.6 18.9 %all-reduce.3 = (f32[2,512,7]{1,0,2:T(2,128)}, f32[32,128]{1,0:T(8,128)}) all-reduce(f32[2,512,7]{1,0,2:T(2,128)S(1)} %constant_dynamic-update-slice_fusion, f32[32,128]{1,0:T(8,128)S(1)} %rev.7), channel_id=1, replica_groups=mesh['dp'=4,'shard'=8] {'dp'}, use_global_device_ids=true, to_apply=%region_8.9 | all-reduce | flops 11264 | bytes 90112 | tf_op jit(solution)/shard_map/psum | solution.py:116
  493.5 12.7 %reduce-scatter.2.cloned.1.call-done = bf16[2048,1024]{0,1:T(8,128)(2,1)} async-done(((bf16[8192,1024]{0,1:T(8,128)(2,1)}), bf16[2048,1024]{0,1:T(8,128)(2,1)}) %reduce-scatter.2.cloned.1.call-update) | async-done | bytes 4194320 | tf_op jit(solution)/shard_map/reduce_scatter | solution.py:121
  506.2 4.0 fusion.52
  510.2 3.9 copy.46
  (67 shorter events, 21.9 us)
Async XLA Ops:
  7.2 93.0 %all-gather.4.cloned.1.call-start = ((), (), s32[]{:S(2)}) async-start(), calls=%async_computation.1 | async-start | bytes 10485760 | tf_op jit(solution)/shard_map/all_gather | solution.py:66
  7.9 1.6 copy-start.6
  7.9 1.8 copy-start.9
  7.9 181.8 %all-gather.6.cloned.1.call-start = ((), (), s32[]{:S(2)}) async-start(), calls=%async_computation.2 | async-start | bytes 10485760 | tf_op jit(solution)/shard_map/all_gather | solution.py:67
  8.7 2.5 copy-start.7
  8.7 264.7 %all-gather.8.cloned.1.call-start = ((), (), s32[]{:S(2)}) async-start(), calls=%async_computation.3 | async-start | bytes 9437184 | tf_op jit(solution)/shard_map/all_gather | solution.py:70
  9.4 496.8 %reduce-scatter.2.cloned.1.call-start = ((), (), s32[]{:S(2)}) async-start(), calls=%async_computation.4 | async-start | bytes 20971520 | tf_op jit(solution)/shard_map/reduce_scatter | solution.py:121
  9.8 52.5 %copy-start.1 = (bf16[2,256,512]{1,2,0:T(8,128)(2,1)}, bf16[2,256,512]{1,2,0:T(8,128)(2,1)S(1)}, u32[]{:S(2)}) copy-start(bf16[2,256,512]{1,2,0:T(8,128)(2,1)S(1)} %broadcast_select_fusion) | copy-start | bytes 1572868
  9.9 52.4 %collective-permute-start.2 = (bf16[2,127,512]{1,2,0:T(8,128)(2,1)S(1)}, bf16[2,127,512]{1,2,0:T(8,128)(2,1)S(1)}, u32[]{:S(2)}, u32[]{:S(2)}) collective-permute-start(bf16[2,127,512]{1,2,0:T(8,128)(2,1)S(1)} %slice.152), channel_id=1, source_target_pairs={{8,0},{16,8},{24,16},{9,1},{17,9},{25,17},{10,2},{18,10},{26,18},{... | collective-permute-start | bytes 780296 | tf_op jit(solution)/shard_map/ppermute | solution.py:10
  43.9 18.4 %copy-start.8 = (f32[2,512,7]{1,0,2:T(2,128)S(1)}, f32[2,512,7]{1,0,2:T(2,128)}, u32[]{:S(2)}) copy-start(f32[2,512,7]{1,0,2:T(2,128)} %param.10) | copy-start | bytes 86020
  287.6 13.7 %copy-start = (bf16[2,256,2,512]{1,0,3,2:T(2,128)(2,1)}, bf16[2,256,2,512]{1,0,3,2:T(2,128)(2,1)S(1)}, u32[]{:S(2)}) copy-start(bf16[2,256,2,512]{1,0,3,2:T(2,128)(2,1)S(1)} %reshape.99) | copy-start | bytes 3145732
  287.6 3.9 copy-start.4
  288.0 15.1 %collective-permute-start = (bf16[2,2,6,512]{2,3,1,0:T(8,128)(2,1)S(1)}, bf16[2,2,6,512]{2,3,1,0:T(8,128)(2,1)S(1)}, u32[]{:S(2)}, u32[]{:S(2)}) collective-permute-start(bf16[2,2,6,512]{2,3,1,0:T(8,128)(2,1)S(1)} %slice.137), channel_id=1, source_target_pairs={{0,8},{8,16},{16,24},{1,9},{9,17},{17,25},{2,10},{10,18},{18,26},{... | collective-permute-start | bytes 73736 | tf_op jit(solution)/shard_map/ppermute | solution.py:10
  303.1 4.9 copy-start.5
  310.6 6.5 %collective-permute-start.3 = (f32[2,2,6,512]{3,1,2,0:T(2,128)S(1)}, f32[2,2,6,512]{3,1,2,0:T(2,128)S(1)}, u32[]{:S(2)}, u32[]{:S(2)}) collective-permute-start(f32[2,2,6,512]{3,1,2,0:T(2,128)S(1)} %copy.42), channel_id=1, source_target_pairs={{8,0},{16,8},{24,16},{9,1},{17,9},{25,17},{10,2},{18,10},{26,18},{... | collective-permute-start | bytes 147464 | tf_op jit(solution)/shard_map/ppermute | solution.py:10
  398.4 16.4 %copy-start.3 = (bf16[2,256,512]{1,2,0:T(8,128)(2,1)S(1)}, bf16[2,256,512]{1,2,0:T(8,128)(2,1)}, u32[]{:S(2)}) copy-start(bf16[2,256,512]{1,2,0:T(8,128)(2,1)} %get-tuple-element.43) | copy-start | bytes 1572868
  398.4 16.8 %copy-start.2 = (bf16[2,256,512]{1,2,0:T(8,128)(2,1)S(1)}, bf16[2,256,512]{1,2,0:T(8,128)(2,1)}, u32[]{:S(2)}) copy-start(bf16[2,256,512]{1,2,0:T(8,128)(2,1)} %copy-done.1) | copy-start | bytes 1572868
  398.4 16.3 %collective-permute-start.1 = (bf16[2,127,512]{1,2,0:T(8,128)(2,1)S(1)}, bf16[2,127,512]{1,2,0:T(8,128)(2,1)S(1)}, u32[]{:S(2)}, u32[]{:S(2)}) collective-permute-start(bf16[2,127,512]{1,2,0:T(8,128)(2,1)S(1)} %slice.150), channel_id=1, source_target_pairs={{0,8},{8,16},{16,24},{1,9},{9,17},{17,25},{2,10},{10,18},{18,26},{... | collective-permute-start | bytes 780296 | tf_op jit(solution)/shard_map/ppermute | solution.py:10
Sparse Core Ops, SparseCore 0:
  9.8 90.2 all-gather.3
  102.0 87.5 all-gather.5
  191.3 82.0 all-gather.7
  346.3 159.8 reduce-scatter.1
where the time goes:
time: 532 us; the launch traced here: 524 us
  waiting for transfers between devices  237 us (45%)
  local copies, waits for them, and re-layouts  159 us (30%)
  matrix products  57.3 us (11%)
  other arithmetic  25.8 us (5%)
  blocking collectives  18.9 us (4%)
  between operations  14.6 us (3%)
  starting transfers between devices  11.1 us (2%)
    all_gather x1, waiting for transfers between devices, shards(): lax.all_gather(value_panel, 'dp', axis=0, tiled=True)  89.5 us
    all_gather x1, waiting for transfers between devices, shards(): features = lax.all_gather(inputs, 'shard', axis=2, tiled=True)  83.7 us
    unnamed x34, local copies, waits for them, and re-layouts  55.4 us
    all_gather x1, waiting for transfers between devices, shards(): lax.all_gather(key_panel, 'dp', axis=0, tiled=True)  36.9 us
    reshape x2, local copies, waits for them, and re-layouts, band(): return tiled.reshape(groups, count, width)  36.7 us
    slice x2, local copies, waits for them, and re-layouts, band(): tiled = jnp.tile(padded, (1, count))[:, :count * width]  20.4 us
    psum x1, blocking collectives, shards(): short_grad, medium_grad = lax.psum((short_local, medium_local), 'dp')  18.9 us
    dot_general x1, matrix products, shards(): lax.dot_general(flat_features, outgoing, (((0,), (0,)), ((), ())), prefer...  15.9 us
  transfers between devices with their start and end apart: 8, of which 7 were waited for; matrix products, arithmetic and copies ran while one was open for 34% of the time, Pallas kernels for 0%

commit v1 on v0

--- a/solution.py
+++ b/solution.py
@@ -1,7 +1,13 @@
+import functools
+
 import jax
 import jax.numpy as jnp
 from jax import lax
+from jax.experimental import pallas as pl
+from jax.experimental.pallas import tpu as pltpu
 from jax.sharding import PartitionSpec as P
+
+BLOCK = 128
 
 
 def shifted(value, axis, steps):
@@ -55,7 +61,7 @@
     return jnp.stack(columns, axis=-1)
 
 
-def shards(inputs, key_panel, value_panel, short_filters, medium_filters, lengths, cotangent):
+def by_positions(inputs, key_panel, value_panel, short_filters, medium_filters, lengths, cotangent):
     seqs, count, local_width = inputs.shape
     channels = key_panel.shape[1]
     groups, taps = medium_filters.shape
@@ -131,6 +137,264 @@
     return (mixed, key_grad, value_grad, short_grad, medium_grad)
 
 
+def hyena_kernel(
+    taps,
+    group,
+    lengths_ref,
+    keys_ref,
+    values_ref,
+    cot_ref,
+    short_ref,
+    medium_ref,
+    reversed_ref,
+    mixed_ref,
+    key_act_ref,
+    value_act_ref,
+    short_grad_ref,
+    sums_ref,
+    pad_ref,
+    smooth_ref,
+    grad_ref,
+    product_ref,
+    upstream_ref,
+    ahead_band,
+    behind_band,
+    corr_ref,
+    short_acc,
+):
+    blocks, seqs, count, lanes = keys_ref.shape
+    halves = count // BLOCK
+    steps = blocks * halves
+    length = blocks * count
+    groups = lanes // group
+    wide = seqs * lanes
+
+    for g in range(groups):
+        rows = pl.ds(g * BLOCK, BLOCK)
+        base = jnp.broadcast_to(reversed_ref[g : g + 1, :], (BLOCK, 2 * BLOCK))
+        behind_band[rows, :] = pltpu.roll(base, 0, 1, stride=1, stride_axis=0).astype(jnp.bfloat16)
+        base = jnp.broadcast_to(medium_ref[g : g + 1, :], (BLOCK, 2 * BLOCK))
+        ahead_band[rows, :] = pltpu.roll(base, 0, 1, stride=1, stride_axis=0).astype(jnp.bfloat16)
+
+    zeros8 = jnp.zeros((8, lanes), jnp.float32)
+    zeros_block = jnp.zeros((BLOCK, lanes), jnp.bfloat16)
+    for s in range(seqs):
+        for branch in range(2):
+            pad_ref[branch, s, pl.ds(0, 8), :] = zeros8
+            grad_ref[branch, s, pl.ds(length, 8), :] = zeros8
+        product_ref[pl.ds(0, BLOCK), pl.ds(s * lanes, lanes)] = zeros_block
+        upstream_ref[pl.ds(length, BLOCK), pl.ds(s * lanes, lanes)] = zeros_block
+
+    def smooth(step, carry):
+        block, half = step // halves, step % halves
+        source = pl.ds(pl.multiple_of(half * BLOCK, BLOCK), BLOCK)
+        begin = pl.multiple_of(step * BLOCK, BLOCK)
+        place = lax.broadcasted_iota(jnp.int32, (BLOCK, lanes), 0) + begin
+        for s in range(seqs):
+            parts = []
+            for branch, ref in ((0, keys_ref), (1, values_ref)):
+                now = ref[block, s, source, :].astype(jnp.float32)
+                pad_ref[branch, s, pl.ds(begin + 8, BLOCK), :] = now
+                window = pad_ref[branch, s, pl.ds(begin, BLOCK + 8), :]
+                total = short_ref[branch, 0:1, :] * now
+                for tap in range(1, taps):
+                    total += short_ref[branch, tap : tap + 1, :] * window[8 - tap : 8 - tap + BLOCK]
+                smooth_ref[branch, s, pl.ds(begin, BLOCK), :] = total
+                parts.append(total)
+            columns = pl.ds(s * lanes, lanes)
+            product_ref[pl.ds(begin + BLOCK, BLOCK), columns] = (parts[0] * parts[1]).astype(
+                jnp.bfloat16
+            )
+            cot = cot_ref[block, s, source, :].astype(jnp.float32)
+            upstream_ref[pl.ds(begin, BLOCK), columns] = jnp.where(
+                place < lengths_ref[s], cot, 0.0
+            ).astype(jnp.bfloat16)
+        return carry
+
+    lax.fori_loop(0, steps, smooth, 0)
+
+    lane_group = lax.broadcasted_iota(jnp.int32, (BLOCK, wide), 1) % lanes // group
+    corr_ref[...] = jnp.zeros_like(corr_ref)
+    short_acc[...] = jnp.zeros_like(short_acc)
+
+    def own(stacked):
+        chosen = stacked[0:BLOCK]
+        for g in range(1, groups):
+            chosen = jnp.where(lane_group == g, stacked[g * BLOCK : (g + 1) * BLOCK], chosen)
+        return chosen
+
+    def mix(step, carry):
+        block, half = step // halves, step % halves
+        source = pl.ds(pl.multiple_of(half * BLOCK, BLOCK), BLOCK)
+        begin = pl.multiple_of(step * BLOCK, BLOCK)
+        place = lax.broadcasted_iota(jnp.int32, (BLOCK, lanes), 0) + begin
+        past = product_ref[pl.ds(begin, 2 * BLOCK), :]
+        response = own(jnp.dot(behind_band[...], past, preferred_element_type=jnp.float32))
+        future = upstream_ref[pl.ds(begin, 2 * BLOCK), :]
+        product_grad = own(jnp.dot(ahead_band[...], future, preferred_element_type=jnp.float32))
+        here = future[0:BLOCK]
+        apart = jnp.concatenate(
+            [jnp.where(lane_group == g, here, jnp.zeros_like(here)) for g in range(groups)], axis=0
+        )
+        corr_ref[...] += lax.dot_general(
+            apart, past, (((1,), (1,)), ((), ())), preferred_element_type=jnp.float32
+        )
+        for s in range(seqs):
+            columns = slice(s * lanes, (s + 1) * lanes)
+            mixed_ref[block, s, source, :] = jnp.where(
+                place < lengths_ref[s], response[:, columns], 0.0
+            ).astype(jnp.bfloat16)
+            for branch in range(2):
+                grad = product_grad[:, columns] * smooth_ref[1 - branch, s, pl.ds(begin, BLOCK), :]
+                grad_ref[branch, s, pl.ds(begin, BLOCK), :] = grad
+                window = pad_ref[branch, s, pl.ds(begin, BLOCK + 8), :]
+                for tap in range(taps):
+                    term = grad * window[8 - tap : 8 - tap + BLOCK]
+                    short_acc[branch, tap] += jnp.sum(term.reshape(BLOCK // 8, 8, lanes), axis=0)
+        return carry
+
+    lax.fori_loop(0, steps, mix, 0)
+
+    def back(step, carry):
+        block, half = step // halves, step % halves
+        source = pl.ds(pl.multiple_of(half * BLOCK, BLOCK), BLOCK)
+        begin = pl.multiple_of(step * BLOCK, BLOCK)
+        for s in range(seqs):
+            for branch, ref in ((0, key_act_ref), (1, value_act_ref)):
+                window = grad_ref[branch, s, pl.ds(begin, BLOCK + 8), :]
+                total = short_ref[branch, 0:1, :] * window[0:BLOCK]
+                for tap in range(1, taps):
+                    total += short_ref[branch, tap : tap + 1, :] * window[tap : tap + BLOCK]
+                ref[block, s, source, :] = total.astype(jnp.bfloat16)
+        return carry
+
+    lax.fori_loop(0, steps, back, 0)
+
+    for branch in range(2):
+        for tap in range(8):
+            if tap < taps:
+                short_grad_ref[branch, tap : tap + 1, :] = jnp.sum(
+                    short_acc[branch, tap], axis=0, keepdims=True
+                )
+            else:
+                short_grad_ref[branch, tap : tap + 1, :] = jnp.zeros((1, lanes), jnp.float32)
+    for g in range(groups):
+        rows = BLOCK
+        total = corr_ref[pl.ds(g * BLOCK, BLOCK), :]
+        while rows > 1:
+            rows //= 2
+            total = total[:rows] + pltpu.roll(total[rows:], 2 * BLOCK - rows, 1)
+        sums_ref[g : g + 1, :] = total
+
+
+def hyena(keys, values, cotangent, short_filters, medium_filters, lengths):
+    blocks, seqs, count, lanes = keys.shape
+    groups, medium = medium_filters.shape
+    taps = short_filters.shape[-1]
+    length = blocks * count
+    short = jnp.pad(short_filters.transpose(0, 2, 1), ((0, 0), (0, 8 - taps), (0, 0)))
+    forward = jnp.pad(medium_filters, ((0, 0), (0, 2 * BLOCK - medium)))
+    backward = jnp.pad(
+        medium_filters[:, ::-1], ((0, 0), (BLOCK + 1 - medium, BLOCK - 1))
+    )
+    vmem = pl.BlockSpec(memory_space=pltpu.VMEM)
+    acts = jax.ShapeDtypeStruct(keys.shape, jnp.bfloat16)
+    mixed, key_act, value_act, short_grad, sums = pl.pallas_call(
+        functools.partial(hyena_kernel, taps, lanes // groups),
+        out_shape=(
+            acts,
+            acts,
+            acts,
+            jax.ShapeDtypeStruct((2, 8, lanes), jnp.float32),
+            jax.ShapeDtypeStruct((groups, 2 * BLOCK), jnp.float32),
+        ),
+        in_specs=[pl.BlockSpec(memory_space=pltpu.SMEM)] + [vmem] * 6,
+        out_specs=[vmem] * 5,
+        scratch_shapes=[
+            pltpu.VMEM((2, seqs, length + 8, lanes), jnp.float32),
+            pltpu.VMEM((2, seqs, length, lanes), jnp.float32),
+            pltpu.VMEM((2, seqs, length + 8, lanes), jnp.float32),
+            pltpu.VMEM((length + BLOCK, seqs * lanes), jnp.bfloat16),
+            pltpu.VMEM((length + BLOCK, seqs * lanes), jnp.bfloat16),
+            pltpu.VMEM((groups * BLOCK, 2 * BLOCK), jnp.bfloat16),
+            pltpu.VMEM((groups * BLOCK, 2 * BLOCK), jnp.bfloat16),
+            pltpu.VMEM((groups * BLOCK, 2 * BLOCK), jnp.float32),
+            pltpu.VMEM((2, taps, 8, lanes), jnp.float32),
+        ],
+        compiler_params=pltpu.CompilerParams(vmem_limit_bytes=40 * 1024 * 1024),
+        cost_estimate=pl.CostEstimate(
+            flops=12 * groups * length * seqs * 2 * BLOCK * lanes,
+            bytes_accessed=12 * length * seqs * lanes,
+            transcendentals=0,
+        ),
+    )(lengths, keys, values, cotangent, short, forward, backward)
+    medium_grad = sums[:, BLOCK - medium + 1 : BLOCK + 1][:, ::-1]
+    return mixed, key_act, value_act, short_grad[:, :taps].transpose(0, 2, 1), medium_grad
+
+
+def by_channels(inputs, key_panel, value_panel, short_filters, medium_filters, lengths, cotangent):
+    seqs, count, width = inputs.shape
+    blocks = lax.axis_size("dp")
+    shard = lax.axis_size("shard")
+    channels = key_panel.shape[1]
+    lanes = channels // blocks
+    groups = medium_filters.shape[0] // blocks
+    mine = lax.axis_index("dp")
+    cores = shard // blocks
+    across = [[b * cores + core for b in range(blocks)] for core in range(cores)]
+    paired = [[b * cores + core for core in range(cores)] for b in range(blocks)]
+    spread = lax.all_gather(inputs, "shard", axis_index_groups=across)
+    turned = lax.all_to_all(spread, "dp", split_axis=0, concat_axis=0, tiled=True)
+    features = lax.all_gather(turned, "shard", axis_index_groups=paired)
+    features = features.reshape(cores, blocks * seqs * count, width)
+    cot = lax.all_to_all(
+        cotangent.reshape(seqs, count, blocks, lanes), "dp", split_axis=2, concat_axis=0
+    )
+
+    def project(panel):
+        partial = jnp.einsum(
+            "cnf,cfm->nm",
+            features,
+            panel.reshape(cores, width, channels),
+            preferred_element_type=jnp.float32,
+        ).astype(jnp.bfloat16)
+        owned = lax.psum_scatter(partial, "dp", scatter_dimension=1, tiled=True)
+        return owned.reshape(blocks, seqs, count, lanes)
+
+    keys, values = project(key_panel), project(value_panel)
+    short = lax.dynamic_slice_in_dim(short_filters, mine * lanes, lanes, 1)
+    medium = lax.dynamic_slice_in_dim(medium_filters, mine * groups, groups, 0)
+    mixed, key_act, value_act, short_grad, medium_grad = hyena(
+        keys, values, cot, short, medium, lengths
+    )
+
+    def panel_grad(act):
+        gathered = lax.all_gather(act.reshape(-1, lanes), "dp", axis=1, tiled=True)
+        return (
+            jnp.einsum("cnf,nm->cfm", features, gathered, preferred_element_type=jnp.float32)
+            .astype(jnp.bfloat16)
+            .reshape(cores * width, channels)
+        )
+
+    key_grad, value_grad = panel_grad(key_act), panel_grad(value_act)
+    mixed = lax.all_to_all(mixed, "dp", split_axis=0, concat_axis=2, tiled=False)
+    mixed = mixed.reshape(seqs, count, channels)
+    short_grad = lax.all_gather(short_grad, "dp", axis=1, tiled=True)
+    medium_grad = lax.all_gather(medium_grad, "dp", axis=0, tiled=True)
+    return (mixed, key_grad, value_grad, short_grad, medium_grad)
+
+
+def shards(inputs, key_panel, value_panel, short_filters, medium_filters, lengths, cotangent):
+    blocks, shard = lax.axis_size("dp"), lax.axis_size("shard")
+    channels = key_panel.shape[1]
+    whole_lanes = channels % (blocks * BLOCK) == 0
+    whole_rows = shard % blocks == 0 and inputs.shape[1] % BLOCK == 0
+    plan = by_channels if whole_lanes and whole_rows else by_positions
+    return plan(
+        inputs, key_panel, value_panel, short_filters, medium_filters, lengths, cotangent
+    )
+
+
 def solution(mesh):
     return jax.shard_map(
         shards,

time: 532 us -> 368 us (0.69); the launches traced: 524 us -> 367 us
  local copies, waits for them, and re-layouts: 159 us -> 32.3 us
  blocking collectives: 18.9 us -> 76.3 us
  waiting for transfers between devices: 237 us -> 186 us
  other arithmetic: 25.8 us -> 0 us
  matrix products: 57.3 us -> 38.6 us
  Pallas kernels: 0 us -> 12.2 us
    all_gather x3 -> x4, waiting for transfers between devices: 210 us -> 134 us  [the longest x1 85.1 us: by_channels(): spread = lax.all_gather(inputs, 'shard', axis_index_groups=across)]
    all_to_all x0 -> x1, blocking collectives: none -> 53.8 us  [by_channels(): lax.all_to_all(spread, 'dp', split_axis=0, concat_axis=0, tiled=True)]
    unnamed x4 -> x8, waiting for transfers between devices: 2.07 us -> 52 us
    reshape x5 -> x2, local copies, waits for them, and re-layouts: 50.4 us -> 3.11 us  [panel_grad(): gathered = lax.all_gather(act.reshape(-1, lanes), 'dp', axis=1, tiled=True)]
    unnamed x34 -> x21, local copies, waits for them, and re-layouts: 55.4 us -> 18.4 us
    slice x8 -> x1, local copies, waits for them, and re-layouts: 27.3 us -> 0.07 us  [hyena(): medium_grad = sums[:, BLOCK - medium + 1:BLOCK + 1][:, ::-1]]
    all_gather x0 -> x2, blocking collectives: none -> 22.5 us  [the longest x1 13.5 us: by_channels(): short_grad = lax.all_gather(short_grad, 'dp', axis=1, tiled=True)]
    psum x1 -> x0, blocking collectives: 18.9 us -> none  [shards(): short_grad, medium_grad = lax.psum((short_local, medium_local), 'dp')]
  transfers between devices with their start and end apart: 8 -> 8, of which waited for: 7 -> 6; matrix products, arithmetic and copies ran while one was open for 34% -> 10% of each run, Pallas kernels for 0% -> 0%
where the time goes in v1:
time: 368 us; the launch traced here: 367 us
  waiting for transfers between devices  186 us (51%)
  blocking collectives  76.3 us (21%)
  matrix products  38.6 us (10%)
  local copies, waits for them, and re-layouts  32.3 us (9%)
  between operations  14.2 us (4%)
  Pallas kernels  12.2 us (3%)
  starting transfers between devices  7.63 us (2%)
    all_gather x1, waiting for transfers between devices, by_channels(): spread = lax.all_gather(inputs, 'shard', axis_index_groups=across)  85.1 us
    all_to_all x1, blocking collectives, by_channels(): lax.all_to_all(spread, 'dp', split_axis=0, concat_axis=0, tiled=True)  53.8 us
    unnamed x8, waiting for transfers between devices  52 us
    all_gather x2, waiting for transfers between devices, panel_grad(): gathered = lax.all_gather(act.reshape(-1, lanes), 'dp', axis=1, tiled=True)  32.3 us
    dot_general x2, matrix products, panel_grad(): jnp.einsum('cnf,nm->cfm', features, gathered, preferred_element_type=jnp....  19.7 us
    dot_general x2, matrix products, project(): jnp.einsum('cnf,cfm->nm', features, panel.reshape(cores, width, channels)...  18.9 us
    unnamed x21, local copies, waits for them, and re-layouts  18.4 us
    all_gather x1, waiting for transfers between devices, by_channels(): features = lax.all_gather(turned, 'shard', axis_index_groups=paired)  17 us
  transfers between devices with their start and end apart: 8, of which 6 were waited for; matrix products, arithmetic and copies ran while one was open for 10% of the time, Pallas kernels for 0%

profile of v1, /device:TPU:0, one launch (start us, length us, event | category | flops | bytes accessed | tf_op | source)
XLA Modules:
  0.0 367.5 jit_solution(17550431809446259253)
XLA Ops:
  8.0 85.1 %all-gather.11.cloned.1.call-done = bf16[8,256,1024]{2,1,0:T(8,128)(2,1)} async-done(((bf16[2,256,1024]{2,1,0:T(8,128)(2,1)}), bf16[8,256,1024]{2,1,0:T(8,128)(2,1)}) %all-gather.11.cloned.1.call-update) | async-done | bytes 4194320 | tf_op jit(solution)/shard_map/all_gather | solution.py:346
  93.1 53.8 %all_to_all.35 = bf16[4,2,256,1024]{3,2,1,0:T(8,128)(2,1)} all-to-all(bf16[4,2,256,1024]{3,2,1,0:T(8,128)(2,1)} %bitcast.65), channel_id=1, replica_groups=mesh['dp'=4,'shard'=8] {'dp'}, dimensions={0} | all-to-all | bytes 8388608 | tf_op jit(solution)/shard_map/all_to_all | solution.py:347
  147.0 17.0 %all-gather.13.cloned.1.call-done = bf16[8,2,256,1024]{3,2,1,0:T(8,128)(2,1)} async-done(((bf16[4,2,256,1024]{3,2,1,0:T(8,128)(2,1)}), bf16[8,2,256,1024]{3,2,1,0:T(8,128)(2,1)}) %all-gather.13.cloned.1.call-update) | async-done | bytes 8388624 | tf_op jit(solution)/shard_map/all_gather | solution.py:348
  164.0 9.1 %bitcast_convert_fusion.1 = bf16[2048,512]{1,0:T(8,128)(2,1)} fusion(bf16[2,2048,1024]{2,1,0:T(8,128)(2,1)} %bitcast.73, bf16[2,1024,512]{2,1,0:T(8,128)(2,1)S(1)} %bitcast.57), kind=kOutput, calls=%fused_computation.1 | convolution fusion | flops 4296015872 | bytes 12582912 | tf_op jit(solution)/shard_map/cnf,cfm->nm/dot_general | solution.py:355
  173.0 3.9 %copy.37 = bf16[2048,512]{0,1:T(8,128)(2,1)} copy(bf16[2048,512]{1,0:T(8,128)(2,1)} %bitcast_convert_fusion.1) | data formatting | bytes 4194304
  177.0 9.8 %bitcast_convert_fusion = bf16[2048,512]{1,0:T(8,128)(2,1)} fusion(bf16[2,2048,1024]{2,1,0:T(8,128)(2,1)} %bitcast.74, bf16[2,1024,512]{2,1,0:T(8,128)(2,1)} %bitcast.77), kind=kOutput, calls=%fused_computation | convolution fusion | flops 4296015872 | bytes 12582912 | tf_op jit(solution)/shard_map/cnf,cfm->nm/dot_general | solution.py:355
  186.8 4.0 %copy.39 = bf16[2048,512]{0,1:T(8,128)(2,1)} copy(bf16[2048,512]{1,0:T(8,128)(2,1)} %bitcast_convert_fusion) | data formatting | bytes 4194304
  190.9 1.0 copy-done.5
  192.1 1.0 copy.27
  193.1 3.9 %all-to-all-start.1 = ((bf16[1,2,256,4,128]{4,2,1,0,3:T(8,128)(2,1)}), bf16[1,2,256,4,128]{4,2,1,0,3:T(8,128)(2,1)S(1)}, u32[]{:S(2)}, u32[]{:S(2)}) async-start(bf16[1,2,256,4,128]{4,2,1,0,3:T(8,128)(2,1)} %copy.27), calls=%async_computation.1 | async-start | bytes 1048576 | tf_op jit(solution)/shard_map/all_to_all | solution.py:350
  197.1 0.7 constant_dynamic-slice_fusion
  197.9 0.7 constant_dynamic-slice_fusion.1
  198.6 14.9 %reduce-scatter.7.cloned.1.call-done = bf16[128,2048]{1,0:T(8,128)(2,1)} async-done(((bf16[512,2048]{1,0:T(8,128)(2,1)}), bf16[128,2048]{1,0:T(8,128)(2,1)}) %reduce-scatter.7.cloned.1.call-update) | async-done | bytes 524304
  213.5 2.0 copy.38
  215.6 36.3 %reduce-scatter.9.cloned.1.call-done = bf16[128,2048]{1,0:T(8,128)(2,1)} async-done(((bf16[512,2048]{1,0:T(8,128)(2,1)}), bf16[128,2048]{1,0:T(8,128)(2,1)}) %reduce-scatter.9.cloned.1.call-update) | async-done | bytes 524304
  251.8 2.0 copy.40
  253.9 1.0 copy-done.1
  254.9 1.0 copy-done.2
  256.0 12.2 %shard_map.110 = (bf16[4,2,256,128]{3,2,1,0:T(8,128)(2,1)}, bf16[4,2,256,128]{3,2,1,0:T(8,128)(2,1)S(1)}, bf16[4,2,256,128]{3,2,1,0:T(8,128)(2,1)S(1)}, f32[2,8,128]{2,1,0:T(8,128)S(1)}, f32[8,256]{1,0:T(8,128)S(1)}) custom-call(s32[2]{0:T(128)S(1)} %copy-done.4, bf16[4,2,256,128]{3,2,1,0:T(8,128)(2,1)S(1)} %bitcast.60, ...), custom_call_target="tpu_custom_call" | custom-call | flops 6442450944 | bytes 3145728 | tf_op jit(solution)/shard_map/pallas_call | solution.py:302
  268.1 0.8 copy-done.3
  268.9 2.0 copy.31
  271.0 1.1 copy.33
  272.1 3.5 all-to-all-start.2
  275.6 13.5 %all_gather.30 = f32[2,512,7]{1,2,0:T(8,128)S(1)} all-gather(f32[2,128,7]{1,2,0:T(8,128)S(1)} %slice_bitcast_fusion), channel_id=1, replica_groups=mesh['dp'=4,'shard'=8] {'dp'}, dimensions={1}, use_global_device_ids=true | all-gather | bytes 35840 | tf_op jit(solution)/shard_map/all_gather | solution.py:382
  290.0 9.0 %all_gather.31 = f32[32,128]{1,0:T(8,128)S(1)} all-gather(f32[8,128]{1,0:T(8,128)S(1)} %rev.7), channel_id=1, replica_groups=mesh['dp'=4,'shard'=8] {'dp'}, dimensions={0}, use_global_device_ids=true | all-gather | bytes 20480 | tf_op jit(solution)/shard_map/all_gather | solution.py:383
  299.2 1.0 copy.35
  300.2 9.0 %all-gather.7.cloned.1.call-done = bf16[2048,512]{0,1:T(8,128)(2,1)} async-done(((bf16[2048,128]{0,1:T(8,128)(2,1)}), bf16[2048,512]{0,1:T(8,128)(2,1)}) %all-gather.7.cloned.1.call-update) | async-done | bytes 2097168 | tf_op jit(solution)/shard_map/all_gather | solution.py:372
  309.2 9.8 %convert_bitcast_fusion.1 = bf16[2,1024,512]{1,2,0:T(8,128)(2,1)} fusion(bf16[2,2048,1024]{2,1,0:T(8,128)(2,1)} %bitcast.75, bf16[2048,512]{0,1:T(8,128)(2,1)} %all-gather.7.cloned.1.call-done), kind=kOutput, calls=%fused_computation.7 | convolution fusion | flops 4296015872 | bytes 12582912 | tf_op jit(solution)/shard_map/cnf,nm->cfm/dot_general | solution.py:374
  319.0 4.0 %copy.32 = bf16[2,1024,512]{2,1,0:T(8,128)(2,1)} copy(bf16[2,1024,512]{1,2,0:T(8,128)(2,1)} %convert_bitcast_fusion.1) | data formatting | bytes 4194304 | tf_op jit(solution)/shard_map/convert_element_type | solution.py:375
  323.0 23.2 %all-gather.9.cloned.1.call-done = bf16[2048,512]{0,1:T(8,128)(2,1)} async-done(((bf16[2048,128]{0,1:T(8,128)(2,1)}), bf16[2048,512]{0,1:T(8,128)(2,1)}) %all-gather.9.cloned.1.call-update) | async-done | bytes 2097168 | tf_op jit(solution)/shard_map/all_gather | solution.py:372
  346.2 9.9 %convert_bitcast_fusion = bf16[2,1024,512]{1,2,0:T(8,128)(2,1)} fusion(bf16[2,2048,1024]{2,1,0:T(8,128)(2,1)} %bitcast.76, bf16[2048,512]{0,1:T(8,128)(2,1)} %all-gather.9.cloned.1.call-done), kind=kOutput, calls=%fused_computation.6 | convolution fusion | flops 4296015872 | bytes 12582912 | tf_op jit(solution)/shard_map/cnf,nm->cfm/dot_general | solution.py:374
  356.1 3.9 %copy.34 = bf16[2,1024,512]{2,1,0:T(8,128)(2,1)} copy(bf16[2,1024,512]{1,2,0:T(8,128)(2,1)} %convert_bitcast_fusion) | data formatting | bytes 4194304 | tf_op jit(solution)/shard_map/convert_element_type | solution.py:375
  (34 shorter events, 3.0 us)
Async XLA Ops:
  7.2 156.8 %copy-start = (bf16[2048,512]{1,0:T(8,128)(2,1)S(1)}, bf16[2048,512]{1,0:T(8,128)(2,1)}, u32[]{:S(2)}) copy-start(bf16[2048,512]{1,0:T(8,128)(2,1)} %param.8) | copy-start | bytes 6291460
  7.2 85.9 %all-gather.11.cloned.1.call-start = ((), (), s32[]{:S(2)}) async-start(), calls=%async_computation.7 | async-start | bytes 5242880 | tf_op jit(solution)/shard_map/all_gather | solution.py:346
  7.9 156.1 %all-gather.13.cloned.1.call-start = ((), (), s32[]{:S(2)}) async-start(), calls=%async_computation.8 | async-start | bytes 12582912 | tf_op jit(solution)/shard_map/all_gather | solution.py:348
  146.9 66.6 %reduce-scatter.7.cloned.1.call-start = ((), (), s32[]{:S(2)}) async-start(), calls=%async_computation.9 | async-start | bytes 2621440
  177.0 74.9 %reduce-scatter.9.cloned.1.call-start = ((), (), s32[]{:S(2)}) async-start(), calls=%async_computation.10 | async-start | bytes 2621440
  190.8 1.1 copy-start.5
  192.1 61.8 %copy-start.4 = (s32[2]{0:T(128)S(1)}, s32[2]{0:T(128)}, u32[]{:S(2)}) copy-start(s32[2]{0:T(128)} %lengths_ref.1) | copy-start | bytes 28
  193.1 60.8 %all-to-all-start.1 = ((bf16[1,2,256,4,128]{4,2,1,0,3:T(8,128)(2,1)}), bf16[1,2,256,4,128]{4,2,1,0,3:T(8,128)(2,1)S(1)}, u32[]{:S(2)}, u32[]{:S(2)}) async-start(bf16[1,2,256,4,128]{4,2,1,0,3:T(8,128)(2,1)} %copy.27), calls=%async_computation.1 | async-start | bytes 1048576 | tf_op jit(solution)/shard_map/all_to_all | solution.py:350
  197.1 112.1 %all-gather.7.cloned.1.call-start = ((), (), s32[]{:S(2)}) async-start(), calls=%async_computation.5 | async-start | bytes 2621440 | tf_op jit(solution)/shard_map/all_gather | solution.py:372
  253.9 1.0 copy-start.1
  254.9 1.0 copy-start.2
  268.1 0.8 copy-start.3
  271.0 75.2 %all-gather.9.cloned.1.call-start = ((), (), s32[]{:S(2)}) async-start(), calls=%async_computation.6 | async-start | bytes 2621440 | tf_op jit(solution)/shard_map/all_gather | solution.py:372
  272.1 26.8 %all-to-all-start.2 = ((bf16[4,2,256,1,128]{4,2,1,3,0:T(8,128)(2,1)}), bf16[4,2,256,1,128]{4,2,1,3,0:T(8,128)(2,1)S(1)}, u32[]{:S(2)}, u32[]{:S(2)}) async-start(bf16[4,2,256,1,128]{4,2,1,3,0:T(8,128)(2,1)} %bitcast.14), calls=%async_computation.2 | async-start | bytes 1048576 | tf_op jit(solution)/shard_map/all_to_all | solution.py:380
Sparse Core Ops, SparseCore 0:
  9.6 83.4 all-gather.10
  147.0 16.9 all-gather.12
  177.1 36.3 reduce-scatter.6
  216.6 35.1 reduce-scatter.8
  271.1 38.0 all-gather.6
  310.9 35.3 all-gather.8

commit v2 on v1

--- a/solution.py
+++ b/solution.py
@@ -162,7 +162,7 @@
     corr_ref,
     short_acc,
 ):
-    blocks, seqs, count, lanes = keys_ref.shape
+    seqs, blocks, count, lanes = keys_ref.shape
     halves = count // BLOCK
     steps = blocks * halves
     length = blocks * count
@@ -193,7 +193,7 @@
         for s in range(seqs):
             parts = []
             for branch, ref in ((0, keys_ref), (1, values_ref)):
-                now = ref[block, s, source, :].astype(jnp.float32)
+                now = ref[s, block, source, :].astype(jnp.float32)
                 pad_ref[branch, s, pl.ds(begin + 8, BLOCK), :] = now
                 window = pad_ref[branch, s, pl.ds(begin, BLOCK + 8), :]
                 total = short_ref[branch, 0:1, :] * now
@@ -265,7 +265,7 @@
                 total = short_ref[branch, 0:1, :] * window[0:BLOCK]
                 for tap in range(1, taps):
                     total += short_ref[branch, tap : tap + 1, :] * window[tap : tap + BLOCK]
-                ref[block, s, source, :] = total.astype(jnp.bfloat16)
+                ref[s, block, source, :] = total.astype(jnp.bfloat16)
         return carry
 
     lax.fori_loop(0, steps, back, 0)
@@ -288,7 +288,7 @@
 
 
 def hyena(keys, values, cotangent, short_filters, medium_filters, lengths):
-    blocks, seqs, count, lanes = keys.shape
+    seqs, blocks, count, lanes = keys.shape
     groups, medium = medium_filters.shape
     taps = short_filters.shape[-1]
     length = blocks * count
@@ -302,7 +302,7 @@
     mixed, key_act, value_act, short_grad, sums = pl.pallas_call(
         functools.partial(hyena_kernel, taps, lanes // groups),
         out_shape=(
-            acts,
+            jax.ShapeDtypeStruct(cotangent.shape, jnp.bfloat16),
             acts,
             acts,
             jax.ShapeDtypeStruct((2, 8, lanes), jnp.float32),
@@ -332,36 +332,370 @@
     return mixed, key_act, value_act, short_grad[:, :taps].transpose(0, 2, 1), medium_grad
 
 
+def remote(source, target, send, recv, dp, shard):
+    return pltpu.make_async_remote_copy(
+        src_ref=source,
+        dst_ref=target,
+        send_sem=send,
+        recv_sem=recv,
+        device_id={"dp": dp, "shard": shard},
+        device_id_type=pl.DeviceIdType.MESH,
+    )
+
+
+def front_kernel(
+    x_ref,
+    key_ref,
+    value_ref,
+    cot_ref,
+    keys_ref,
+    values_ref,
+    cot_out,
+    features_out,
+    line,
+    features,
+    panels,
+    own,
+    outgoing,
+    incoming,
+    cot_in,
+    line_send,
+    line_recv,
+    plane_send,
+    plane_recv,
+    core_send,
+    core_recv,
+    sum_send,
+    sum_recv,
+    cot_send,
+    cot_recv,
+    local,
+    saved,
+):
+    seqs, count, width = x_ref.shape
+    blocks, lanes = cot_in.shape[0], cot_in.shape[-1]
+    rows = count // 2
+    p, shard = lax.axis_index("dp"), lax.axis_index("shard")
+    z, core = shard // 2, shard % 2
+    sibling = z * 2 + (1 - core)
+    peers = [(p + j) % blocks for j in range(blocks)]
+    froms = [(p + blocks - j) % blocks for j in range(blocks)]
+
+    barrier = pltpu.get_barrier_semaphore()
+
+    def greet(dp, to):
+        pl.semaphore_signal(
+            barrier,
+            inc=1,
+            device_id={"dp": dp, "shard": to},
+            device_id_type=pl.DeviceIdType.MESH,
+        )
+
+    greet(p, sibling)
+    for j in range(1, blocks):
+        greet(peers[j], shard)
+
+    for step in (2, 2 * blocks - 2):
+        greet(p, (shard + step) % (2 * blocks))
+    pl.semaphore_wait(barrier, blocks + 2)
+
+    def part(half):
+        return pl.ds(half * rows, rows)
+
+    def held(h, layer, w, half):
+        return x_ref.at[w, part(half)] if h == 0 else line.at[layer, w, part(half)]
+
+    def line_copy(h, layer, w, half, way):
+        piece = w * 2 + half
+        return remote(
+            held(h, layer, w, half),
+            line.at[layer, w, part(half)],
+            line_send.at[way, layer, piece],
+            line_recv.at[layer, piece],
+            p,
+            shard + 2 * (1 - 2 * way),
+        )
+
+    def plane_copy(h, layer, w, half):
+        piece = w * 2 + half
+        return remote(
+            held(h, layer, w, half),
+            features.at[core, w, p, part(half)],
+            plane_send.at[layer, piece],
+            plane_recv.at[p, piece],
+            layer,
+            shard,
+        )
+
+    def plane_arrival(block, w, half):
+        piece = w * 2 + half
+        place = features.at[core, w, block, part(half)]
+        return remote(
+            place, place, plane_send.at[block, piece], plane_recv.at[block, piece], block, shard
+        )
+
+    def core_copy(source, block, w, half):
+        piece = w * 2 + half
+        return remote(
+            source,
+            features.at[core, w, block, part(half)],
+            core_send.at[block, piece],
+            core_recv.at[block, piece],
+            p,
+            sibling,
+        )
+
+    def core_arrival(block, w, half):
+        piece = w * 2 + half
+        place = features.at[1 - core, w, block, part(half)]
+        return remote(
+            place, place, core_send.at[block, piece], core_recv.at[block, piece], p, sibling
+        )
+
+    def keep_copy(h, layer, w, half):
+        return pltpu.make_async_copy(
+            held(h, layer, w, half), features.at[core, w, p, part(half)], local.at[w * 2 + half]
+        )
+
+    def steps(h):
+        if h == 0:
+            return [(0, z, None, z < blocks - 1), (1, z, None, z > 0)]
+        return [
+            (0, z - h, z - h >= 0, z < blocks - 1),
+            (1, z + h, z + h < blocks, z > 0),
+        ]
+
+    def dispatch(h, layer, w, half):
+        @pl.when(layer == p)
+        def _():
+            keep_copy(h, layer, w, half).start()
+            core_copy(held(h, layer, w, half), p, w, half).start()
+
+        @pl.when(layer != p)
+        def _():
+            plane_copy(h, layer, w, half).start()
+
+    def hop(w, h):
+        for half in range(2):
+            if h == 0:
+                for way, layer, _, onward in steps(0):
+
+                    @pl.when(onward)
+                    def _():
+                        line_copy(0, layer, w, half, way).start()
+
+                dispatch(0, z, w, half)
+            else:
+                for way, layer, valid, onward in steps(h):
+
+                    @pl.when(valid)
+                    def _():
+                        line_copy(h, layer, w, half, way).wait_recv()
+
+                        @pl.when(onward)
+                        def _():
+                            line_copy(h, layer, w, half, way).start()
+
+                        dispatch(h, layer, w, half)
+
+    def share(w):
+        for half in range(2):
+            for j in range(1, blocks):
+                plane_arrival(froms[j], w, half).wait_recv()
+                place = features.at[core, w, froms[j], part(half)]
+                core_copy(place, froms[j], w, half).start()
+
+    def save_copy(w):
+        return pltpu.make_async_copy(features.at[:, w], features_out.at[:, w], saved.at[w])
+
+    def complete(w):
+        for half in range(2):
+            for j in range(blocks):
+                core_arrival(froms[j], w, half).wait_recv()
+            keep_copy(0, z, w, half).wait()
+        save_copy(w).start()
+
+    def sum_copy(w, j):
+        return remote(
+            outgoing.at[w, j - 1],
+            incoming.at[w, j - 1],
+            sum_send.at[w, j - 1],
+            sum_recv.at[w, j - 1],
+            peers[j],
+            shard,
+        )
+
+    def project(w, j):
+        def tile(i, carry):
+            total = jnp.zeros((count, 2 * lanes), jnp.float32)
+            for c in range(2):
+                total += jnp.dot(
+                    features[c, w, i], panels[peers[j], c], preferred_element_type=jnp.float32
+                )
+            if j == 0:
+                own[w, i] = total
+            else:
+                outgoing[w, j - 1, i] = total.astype(jnp.bfloat16)
+            return carry
+
+        lax.fori_loop(0, blocks, tile, 0)
+        if j > 0:
+            sum_copy(w, j).start()
+
+    def cot_copy(j):
+        place = pl.ds(pl.multiple_of(peers[j] * lanes, lanes), lanes)
+        return remote(
+            cot_ref.at[:, :, place],
+            cot_in.at[p],
+            cot_send.at[j],
+            cot_recv.at[p],
+            peers[j],
+            shard,
+        )
+
+    def cot_arrival(j):
+        return remote(
+            cot_in.at[froms[j]],
+            cot_in.at[froms[j]],
+            cot_send.at[j],
+            cot_recv.at[froms[j]],
+            froms[j],
+            shard,
+        )
+
+    hop(0, 0)
+    for r in range(blocks):
+        for c in range(2):
+            source = pl.ds(c * width, width)
+            columns = slice(r * lanes, (r + 1) * lanes)
+            panels[r, c, :, 0:lanes] = key_ref[source, columns]
+            panels[r, c, :, lanes : 2 * lanes] = value_ref[source, columns]
+    for h in range(1, blocks):
+        hop(0, h)
+    hop(1, 0)
+    share(0)
+    hop(1, 1)
+    complete(0)
+    project(0, 2)
+    project(0, 1)
+    hop(1, 2)
+    project(0, 3)
+    hop(1, 3)
+    project(0, 0)
+    share(1)
+    for j in range(1, blocks):
+        cot_copy(j).start()
+    cot_in[p] = cot_ref[:, :, pl.ds(pl.multiple_of(p * lanes, lanes), lanes)]
+    complete(1)
+    for j in (1, 3, 2, 0):
+        project(1, j)
+    for j in range(1, blocks):
+        cot_arrival(j).wait_recv()
+    cot_out[...] = cot_in[...]
+    for w in range(seqs):
+        for j in range(1, blocks):
+            sum_copy(w, j).wait_recv()
+
+        def add(i, carry):
+            total = own[w, i]
+            for j in range(1, blocks):
+                total += incoming[w, j - 1, i].astype(jnp.float32)
+            keys_ref[w, i] = total[:, 0:lanes].astype(jnp.bfloat16)
+            values_ref[w, i] = total[:, lanes : 2 * lanes].astype(jnp.bfloat16)
+            return carry
+
+        lax.fori_loop(0, blocks, add, 0)
+
+    for w in range(seqs):
+        save_copy(w).wait()
+        for j in range(1, blocks):
+            sum_copy(w, j).wait_send()
+        for half in range(2):
+            for j in range(blocks):
+                core_copy(features.at[core, w, froms[j], part(half)], froms[j], w, half).wait_send()
+            for h in range(blocks):
+                for way, layer, valid, onward in steps(h):
+                    if h > 0:
+                        onward = jnp.logical_and(valid, onward)
+
+                    @pl.when(onward)
+                    def _():
+                        line_copy(h, layer, w, half, way).wait_send()
+
+                    if h > 0 or way == 0:
+                        sent = layer != p
+                        if h > 0:
+                            sent = jnp.logical_and(valid, sent)
+
+                        @pl.when(sent)
+                        def _():
+                            plane_copy(h, layer, w, half).wait_send()
+
+    for j in range(1, blocks):
+        cot_copy(j).wait_send()
+
+
+def front(inputs, key_panel, value_panel, cotangent, blocks):
+    seqs, count, width = inputs.shape
+    channels = key_panel.shape[1]
+    lanes = channels // blocks
+    pieces = 2 * seqs
+    vmem = pl.BlockSpec(memory_space=pltpu.VMEM)
+    hbm = pl.BlockSpec(memory_space=pl.ANY)
+    acts = jax.ShapeDtypeStruct((seqs, blocks, count, lanes), jnp.bfloat16)
+    feature_shape = (2, seqs, blocks, count, width)
+    dma = pltpu.SemaphoreType.DMA
+    return pl.pallas_call(
+        front_kernel,
+        out_shape=(
+            acts,
+            acts,
+            jax.ShapeDtypeStruct((blocks, seqs, count, lanes), jnp.bfloat16),
+            jax.ShapeDtypeStruct(feature_shape, jnp.bfloat16),
+        ),
+        in_specs=[hbm, vmem, vmem, vmem],
+        out_specs=[vmem, vmem, vmem, hbm],
+        scratch_shapes=[
+            pltpu.VMEM((blocks, seqs, count, width), jnp.bfloat16),
+            pltpu.VMEM(feature_shape, jnp.bfloat16),
+            pltpu.VMEM((blocks, 2, width, 2 * lanes), jnp.bfloat16),
+            pltpu.VMEM((seqs, blocks, count, 2 * lanes), jnp.float32),
+            pltpu.VMEM((seqs, blocks - 1, blocks, count, 2 * lanes), jnp.bfloat16),
+            pltpu.VMEM((seqs, blocks - 1, blocks, count, 2 * lanes), jnp.bfloat16),
+            pltpu.VMEM((blocks, seqs, count, lanes), jnp.bfloat16),
+            dma((2, blocks, pieces)),
+            dma((blocks, pieces)),
+            dma((blocks, pieces)),
+            dma((blocks, pieces)),
+            dma((blocks, pieces)),
+            dma((blocks, pieces)),
+            dma((seqs, blocks - 1)),
+            dma((seqs, blocks - 1)),
+            dma((blocks,)),
+            dma((blocks,)),
+            dma((pieces,)),
+            dma((seqs,)),
+        ],
+        compiler_params=pltpu.CompilerParams(
+            collective_id=0, has_side_effects=True, vmem_limit_bytes=48 * 1024 * 1024
+        ),
+        cost_estimate=pl.CostEstimate(
+            flops=4 * blocks * seqs * count * 2 * width * channels,
+            bytes_accessed=8 * blocks * seqs * count * width,
+            transcendentals=0,
+        ),
+    )(inputs, key_panel, value_panel, cotangent)
+
+
 def by_channels(inputs, key_panel, value_panel, short_filters, medium_filters, lengths, cotangent):
     seqs, count, width = inputs.shape
     blocks = lax.axis_size("dp")
-    shard = lax.axis_size("shard")
     channels = key_panel.shape[1]
     lanes = channels // blocks
     groups = medium_filters.shape[0] // blocks
     mine = lax.axis_index("dp")
-    cores = shard // blocks
-    across = [[b * cores + core for b in range(blocks)] for core in range(cores)]
-    paired = [[b * cores + core for core in range(cores)] for b in range(blocks)]
-    spread = lax.all_gather(inputs, "shard", axis_index_groups=across)
-    turned = lax.all_to_all(spread, "dp", split_axis=0, concat_axis=0, tiled=True)
-    features = lax.all_gather(turned, "shard", axis_index_groups=paired)
-    features = features.reshape(cores, blocks * seqs * count, width)
-    cot = lax.all_to_all(
-        cotangent.reshape(seqs, count, blocks, lanes), "dp", split_axis=2, concat_axis=0
-    )
-
-    def project(panel):
-        partial = jnp.einsum(
-            "cnf,cfm->nm",
-            features,
-            panel.reshape(cores, width, channels),
-            preferred_element_type=jnp.float32,
-        ).astype(jnp.bfloat16)
-        owned = lax.psum_scatter(partial, "dp", scatter_dimension=1, tiled=True)
-        return owned.reshape(blocks, seqs, count, lanes)
-
-    keys, values = project(key_panel), project(value_panel)
+    keys, values, cot, features = front(inputs, key_panel, value_panel, cotangent, blocks)
+    features = features.reshape(2, blocks * seqs * count, width)
     short = lax.dynamic_slice_in_dim(short_filters, mine * lanes, lanes, 1)
     medium = lax.dynamic_slice_in_dim(medium_filters, mine * groups, groups, 0)
     mixed, key_act, value_act, short_grad, medium_grad = hyena(
@@ -373,7 +707,7 @@
         return (
             jnp.einsum("cnf,nm->cfm", features, gathered, preferred_element_type=jnp.float32)
             .astype(jnp.bfloat16)
-            .reshape(cores * width, channels)
+            .reshape(2 * width, channels)
         )
 
     key_grad, value_grad = panel_grad(key_act), panel_grad(value_act)
@@ -387,9 +721,8 @@
 def shards(inputs, key_panel, value_panel, short_filters, medium_filters, lengths, cotangent):
     blocks, shard = lax.axis_size("dp"), lax.axis_size("shard")
     channels = key_panel.shape[1]
-    whole_lanes = channels % (blocks * BLOCK) == 0
-    whole_rows = shard % blocks == 0 and inputs.shape[1] % BLOCK == 0
-    plan = by_channels if whole_lanes and whole_rows else by_positions
+    whole = channels == blocks * BLOCK and inputs.shape[1] % (2 * BLOCK) == 0
+    plan = by_channels if whole and blocks == 4 and shard == 2 * blocks else by_positions
     return plan(
         inputs, key_panel, value_panel, short_filters, medium_filters, lengths, cotangent
     )

time: 368 us -> 264 us (0.72)
  waiting for transfers between devices: 186 us -> 41.6 us
  Pallas kernels: 12.2 us -> 153 us
  blocking collectives: 76.3 us -> 19.7 us
  local copies, waits for them, and re-layouts: 32.3 us -> 7.33 us
  matrix products: 38.6 us -> 19.7 us
    pallas_call x0 -> x1, Pallas kernels: none -> 140 us  [front(): pl.pallas_call(front_kernel, out_shape=(acts, acts, jax.ShapeDtypeStruct(...]
    all_gather x2 -> x0, waiting for transfers between devices: 102 us -> none  [the longest x1 85.1 us: by_channels(): spread = lax.all_gather(inputs, 'shard', axis_index_groups=across)]
    all_to_all x1 -> x0, blocking collectives: 53.8 us -> none  [by_channels(): lax.all_to_all(spread, 'dp', split_axis=0, concat_axis=0, tiled=True)]
    unnamed x8 -> x2, waiting for transfers between devices: 52 us -> 0.71 us
    dot_general x2 -> x0, matrix products: 18.9 us -> none  [project(): jnp.einsum('cnf,cfm->nm', features, panel.reshape(cores, width, channels)...]
    unnamed x21 -> x14, local copies, waits for them, and re-layouts: 18.4 us -> 6.11 us
    all_gather x2, waiting for transfers between devices: 32.3 us -> 40.9 us  [panel_grad(): gathered = lax.all_gather(act.reshape(-1, lanes), 'dp', axis=1, tiled=True)]
    convert_element_type x2 -> x0, local copies, waits for them, and re-layouts: 7.91 us -> none  [panel_grad(): return jnp.einsum('cnf,nm->cfm', features, gathered, preferred_element_ty...]
  transfers between devices with their start and end apart: 8 -> 3, of which waited for: 6 -> 2; matrix products, arithmetic and copies ran while one was open for 10% -> 5% of each run, Pallas kernels for 0% -> 0%
where the time goes in v2:
time: 264 us; the launch traced here: 263 us
  Pallas kernels  153 us (58%)
  waiting for transfers between devices  41.6 us (16%)
  blocking collectives  19.7 us (7%)
  matrix products  19.7 us (7%)
  between operations  14.1 us (5%)
  starting transfers between devices  7.88 us (3%)
  local copies, waits for them, and re-layouts  7.33 us (3%)
    pallas_call x1, Pallas kernels, front(): pl.pallas_call(front_kernel, out_shape=(acts, acts, jax.ShapeDtypeStruct(...  140 us
    all_gather x2, waiting for transfers between devices, panel_grad(): gathered = lax.all_gather(act.reshape(-1, lanes), 'dp', axis=1, tiled=True)  40.9 us
    dot_general x2, matrix products, panel_grad(): jnp.einsum('cnf,nm->cfm', features, gathered, preferred_element_type=jnp....  19.7 us
    pallas_call x1, Pallas kernels, hyena(): pl.pallas_call(functools.partial(hyena_kernel, taps, lanes // groups), ou...  12.6 us
    all_gather x1, blocking collectives, by_channels(): medium_grad = lax.all_gather(medium_grad, 'dp', axis=0, tiled=True)  10.3 us
    all_gather x1, blocking collectives, by_channels(): short_grad = lax.all_gather(short_grad, 'dp', axis=1, tiled=True)  9.45 us
    all_to_all x1, starting transfers between devices, by_channels(): lax.all_to_all(mixed, 'dp', split_axis=0, concat_axis=2, tiled=False)  7.8 us
    unnamed x14, local copies, waits for them, and re-layouts  6.11 us
  transfers between devices with their start and end apart: 3, of which 2 were waited for; matrix products, arithmetic and copies ran while one was open for 5% of the time, Pallas kernels for 0%

profile of v2, /device:TPU:0, one launch (start us, length us, event | category | flops | bytes accessed | tf_op | source)
XLA Modules:
  0.0 263.3 jit_solution(16737421955259520952)
XLA Ops:
  7.2 0.0 copy-start
  7.2 0.0 all-gather.3.cloned.1.call-start
  7.2 0.7 constant_dynamic-slice_fusion
  7.9 0.1 rev.6
  8.0 0.1 pad.14.reversed_ref
  8.1 0.0 copy-done
  8.1 0.0 copy-start.1
  8.1 1.6 copy-done.1
  9.7 0.0 copy-start.2
  9.7 1.2 copy-done.2
  10.9 0.0 copy-start.3
  10.9 1.0 copy-done.3
  12.0 140.3 %shard_map.110 = (bf16[2,4,256,128]{3,2,1,0:T(8,128)(2,1)S(1)}, bf16[2,4,256,128]{3,2,1,0:T(8,128)(2,1)S(1)}, bf16[4,2,256,128]{3,2,1,0:T(8,128)(2,1)S(1)}, bf16[2,2,4,256,1024]{4,3,2,1,0:T(8,128)(2,1)}) custom-call(bf16[2,256,1024]{2,1,0:T(8,128)(2,1)S(1)} %copy-done.2, bf16[2048,512]{1,0:T(8,128)(2,1)S(1)} %copy-done.1, bf16[2048,512]{1,0:T(8,128)(2,1)} %value_ref.1, ...), custom_call_target="tpu_custom_call" | custom-call | flops 8589934592 | bytes 16777216 | tf_op jit(solution)/shard_map/pallas_call | solution.py:648
  152.3 0.0 copy-done.4
  152.3 12.6 %shard_map.111 = (bf16[4,2,256,128]{3,2,1,0:T(8,128)(2,1)}, bf16[2,4,256,128]{3,2,1,0:T(8,128)(2,1)}, bf16[2,4,256,128]{3,2,1,0:T(8,128)(2,1)}, f32[2,8,128]{2,1,0:T(8,128)S(1)}, f32[8,256]{1,0:T(8,128)S(1)}) custom-call(s32[2]{0:T(128)S(1)} %copy-done.4, bf16[2,4,256,128]{3,2,1,0:T(8,128)(2,1)S(1)} %get-tuple-element.14.keys_ref, ...), custom_call_target="tpu_custom_call" | custom-call | flops 6442450944 | bytes 3145728 | tf_op jit(solution)/shard_map/pallas_call | solution.py:302
  164.9 0.0 all-gather.3.cloned.1.call-update
  164.9 0.0 all-gather.5.cloned.1.call-start
  165.0 0.7 all-gather.5.cloned.1.call-update
  165.7 7.8 %all-to-all-start = ((bf16[4,2,256,1,128]{4,2,1,3,0:T(8,128)(2,1)}), bf16[4,2,256,1,128]{4,2,1,3,0:T(8,128)(2,1)S(1)}, u32[]{:S(2)}, u32[]{:S(2)}) async-start(bf16[4,2,256,1,128]{4,2,1,3,0:T(8,128)(2,1)} %bitcast.2), calls=%async_computation | async-start | bytes 1048576 | tf_op jit(solution)/shard_map/all_to_all | solution.py:714
  173.5 0.1 slice.7
  173.6 0.1 rev.7
  173.6 10.3 %all_gather.15 = f32[32,128]{1,0:T(8,128)S(1)} all-gather(f32[8,128]{1,0:T(8,128)S(1)} %rev.7), channel_id=1, replica_groups=mesh['dp'=4,'shard'=8] {'dp'}, dimensions={0}, use_global_device_ids=true | all-gather | bytes 20480 | tf_op jit(solution)/shard_map/all_gather | solution.py:717
  183.9 9.4 %all_gather.14 = f32[2,512,7]{1,2,0:T(8,128)S(1)} all-gather(f32[2,128,7]{1,2,0:T(8,128)S(1)} %slice_bitcast_fusion), channel_id=1, replica_groups=mesh['dp'=4,'shard'=8] {'dp'}, dimensions={1}, use_global_device_ids=true | all-gather | bytes 35840 | tf_op jit(solution)/shard_map/all_gather | solution.py:716
  193.4 0.6 copy.28
  194.0 0.0 all-to-all-done
  194.0 0.2 copy.24
  194.2 1.0 copy.27
  195.2 13.7 %all-gather.3.cloned.1.call-done = bf16[2048,512]{1,0:T(8,128)(2,1)} async-done(((bf16[2048,128]{1,0:T(8,128)(2,1)}), bf16[2048,512]{1,0:T(8,128)(2,1)}) %all-gather.3.cloned.1.call-update) | async-done | bytes 2097168 | tf_op jit(solution)/shard_map/all_gather | solution.py:706
  208.9 9.9 %fusion.4 = bf16[2,1024,512]{2,1,0:T(8,128)(2,1)} fusion(bf16[2,2048,1024]{2,1,0:T(8,128)(2,1)} %bitcast.32, bf16[2048,512]{1,0:T(8,128)(2,1)} %all-gather.3.cloned.1.call-done), kind=kOutput, calls=%fused_computation.4 | convolution fusion | flops 4296015872 | bytes 12582912 | tf_op jit(solution)/shard_map/cnf,nm->cfm/dot_general | solution.py:708
  218.8 27.2 %all-gather.5.cloned.1.call-done = bf16[2048,512]{1,0:T(8,128)(2,1)} async-done(((bf16[2048,128]{1,0:T(8,128)(2,1)}), bf16[2048,512]{1,0:T(8,128)(2,1)}) %all-gather.5.cloned.1.call-update) | async-done | bytes 2097168 | tf_op jit(solution)/shard_map/all_gather | solution.py:706
  246.0 9.9 %fusion.7 = bf16[2,1024,512]{2,1,0:T(8,128)(2,1)} fusion(bf16[2,2048,1024]{2,1,0:T(8,128)(2,1)} %bitcast.33, bf16[2048,512]{1,0:T(8,128)(2,1)} %all-gather.5.cloned.1.call-done), kind=kOutput, calls=%fused_computation.5 | convolution fusion | flops 4296015872 | bytes 12582912 | tf_op jit(solution)/shard_map/cnf,nm->cfm/dot_general | solution.py:708
  255.8 0.6 copy.35
  (6 shorter events, 0.0 us)
Async XLA Ops:
  7.2 0.9 copy-start
  7.2 201.8 %all-gather.3.cloned.1.call-start = ((), (), s32[]{:S(2)}) async-start(), calls=%async_computation.1 | async-start | bytes 2621440 | tf_op jit(solution)/shard_map/all_gather | solution.py:706
  8.1 1.6 copy-start.1
  9.7 1.2 copy-start.2
  10.9 1.0 copy-start.3
  12.0 140.3 %copy-start.4 = (s32[2]{0:T(128)S(1)}, s32[2]{0:T(128)}, u32[]{:S(2)}) copy-start(s32[2]{0:T(128)} %lengths_ref.1) | copy-start | bytes 28
  164.9 81.0 %all-gather.5.cloned.1.call-start = ((), (), s32[]{:S(2)}) async-start(), calls=%async_computation.2 | async-start | bytes 2621440 | tf_op jit(solution)/shard_map/all_gather | solution.py:706
  165.7 28.3 %all-to-all-start = ((bf16[4,2,256,1,128]{4,2,1,3,0:T(8,128)(2,1)}), bf16[4,2,256,1,128]{4,2,1,3,0:T(8,128)(2,1)S(1)}, u32[]{:S(2)}, u32[]{:S(2)}) async-start(bf16[4,2,256,1,128]{4,2,1,3,0:T(8,128)(2,1)} %bitcast.2), calls=%async_computation | async-start | bytes 1048576 | tf_op jit(solution)/shard_map/all_to_all | solution.py:714
Sparse Core Ops, SparseCore 0:
  165.1 43.8 all-gather.2
  210.8 35.1 all-gather.4

commit v3 on v2

--- a/solution.py
+++ b/solution.py
@@ -148,10 +148,8 @@
     medium_ref,
     reversed_ref,
     mixed_ref,
-    key_act_ref,
-    value_act_ref,
-    short_grad_ref,
-    sums_ref,
+    act_ref,
+    small_ref,
     pad_ref,
     smooth_ref,
     grad_ref,
@@ -260,12 +258,13 @@
         source = pl.ds(pl.multiple_of(half * BLOCK, BLOCK), BLOCK)
         begin = pl.multiple_of(step * BLOCK, BLOCK)
         for s in range(seqs):
-            for branch, ref in ((0, key_act_ref), (1, value_act_ref)):
+            for branch in range(2):
                 window = grad_ref[branch, s, pl.ds(begin, BLOCK + 8), :]
                 total = short_ref[branch, 0:1, :] * window[0:BLOCK]
                 for tap in range(1, taps):
                     total += short_ref[branch, tap : tap + 1, :] * window[tap : tap + BLOCK]
-                ref[s, block, source, :] = total.astype(jnp.bfloat16)
+                columns = slice(branch * lanes, (branch + 1) * lanes)
+                act_ref[s, block, source, columns] = total.astype(jnp.bfloat16)
         return carry
 
     lax.fori_loop(0, steps, back, 0)
@@ -273,18 +272,18 @@
     for branch in range(2):
         for tap in range(8):
             if tap < taps:
-                short_grad_ref[branch, tap : tap + 1, :] = jnp.sum(
-                    short_acc[branch, tap], axis=0, keepdims=True
-                )
+                sums = jnp.sum(short_acc[branch, tap], axis=0, keepdims=True)
             else:
-                short_grad_ref[branch, tap : tap + 1, :] = jnp.zeros((1, lanes), jnp.float32)
+                sums = jnp.zeros((1, lanes), jnp.float32)
+            small_ref[branch * 8 + tap : branch * 8 + tap + 1, :] = sums
     for g in range(groups):
         rows = BLOCK
         total = corr_ref[pl.ds(g * BLOCK, BLOCK), :]
         while rows > 1:
             rows //= 2
             total = total[:rows] + pltpu.roll(total[rows:], 2 * BLOCK - rows, 1)
-        sums_ref[g : g + 1, :] = total
+        small_ref[16 + g : 17 + g, :] = total[:, :BLOCK]
+        small_ref[16 + groups + g : 17 + groups + g, :] = total[:, BLOCK:]
 
 
 def hyena(keys, values, cotangent, short_filters, medium_filters, lengths):
@@ -298,18 +297,15 @@
         medium_filters[:, ::-1], ((0, 0), (BLOCK + 1 - medium, BLOCK - 1))
     )
     vmem = pl.BlockSpec(memory_space=pltpu.VMEM)
-    acts = jax.ShapeDtypeStruct(keys.shape, jnp.bfloat16)
-    mixed, key_act, value_act, short_grad, sums = pl.pallas_call(
+    return pl.pallas_call(
         functools.partial(hyena_kernel, taps, lanes // groups),
         out_shape=(
             jax.ShapeDtypeStruct(cotangent.shape, jnp.bfloat16),
-            acts,
-            acts,
-            jax.ShapeDtypeStruct((2, 8, lanes), jnp.float32),
-            jax.ShapeDtypeStruct((groups, 2 * BLOCK), jnp.float32),
+            jax.ShapeDtypeStruct((seqs, blocks, count, 2 * lanes), jnp.bfloat16),
+            jax.ShapeDtypeStruct((16 + 2 * groups, lanes), jnp.float32),
         ),
         in_specs=[pl.BlockSpec(memory_space=pltpu.SMEM)] + [vmem] * 6,
-        out_specs=[vmem] * 5,
+        out_specs=[vmem] * 3,
         scratch_shapes=[
             pltpu.VMEM((2, seqs, length + 8, lanes), jnp.float32),
             pltpu.VMEM((2, seqs, length, lanes), jnp.float32),
@@ -328,8 +324,6 @@
             transcendentals=0,
         ),
     )(lengths, keys, values, cotangent, short, forward, backward)
-    medium_grad = sums[:, BLOCK - medium + 1 : BLOCK + 1][:, ::-1]
-    return mixed, key_act, value_act, short_grad[:, :taps].transpose(0, 2, 1), medium_grad
 
 
 def remote(source, target, send, recv, dp, shard):
@@ -687,6 +681,215 @@
     )(inputs, key_panel, value_panel, cotangent)
 
 
+def back_kernel(
+    act_ref,
+    mixed_ref,
+    small_ref,
+    features_ref,
+    mixed_out,
+    key_out,
+    value_out,
+    small_out,
+    features,
+    turned,
+    got,
+    mixed_in,
+    small_in,
+    act_send,
+    act_recv,
+    mixed_send,
+    mixed_recv,
+    small_send,
+    small_recv,
+    local,
+):
+    seqs, blocks, count, both = act_ref.shape
+    lanes = both // 2
+    width = features.shape[-1]
+    p, shard = lax.axis_index("dp"), lax.axis_index("shard")
+    x, y = p % 2, p // 2
+    beside, above, across = y * 2 + 1 - x, (1 - y) * 2 + x, (1 - y) * 2 + 1 - x
+    owners = (p, beside, above, across)
+
+    loads = [
+        pltpu.make_async_copy(features_ref.at[c], features.at[c], local.at[c]) for c in range(2)
+    ]
+    for load in loads:
+        load.start()
+
+    barrier = pltpu.get_barrier_semaphore()
+    for to in owners[1:]:
+        pl.semaphore_signal(
+            barrier,
+            inc=1,
+            device_id={"dp": to, "shard": shard},
+            device_id_type=pl.DeviceIdType.MESH,
+        )
+    pl.semaphore_wait(barrier, blocks - 1)
+
+    def send_own(slot, w):
+        return remote(
+            act_ref.at[w],
+            got.at[slot - 1, w],
+            act_send.at[slot - 1, w],
+            act_recv.at[slot - 1, w],
+            owners[slot],
+            shard,
+        )
+
+    def pass_on(slot, w):
+        return remote(
+            got.at[slot - 1, w],
+            got.at[2, w],
+            act_send.at[2, w],
+            act_recv.at[2, w],
+            owners[3 - slot],
+            shard,
+        )
+
+    def arrived(slot, w):
+        place = got.at[slot - 1, w]
+        return remote(
+            place,
+            place,
+            act_send.at[slot - 1, w],
+            act_recv.at[slot - 1, w],
+            owners[slot],
+            shard,
+        )
+
+    def mixed_copy(k):
+        return remote(
+            mixed_ref.at[owners[k]],
+            mixed_in.at[k - 1],
+            mixed_send.at[k - 1],
+            mixed_recv.at[k - 1],
+            owners[k],
+            shard,
+        )
+
+    def small_copy(k):
+        return remote(
+            small_ref,
+            small_in.at[k - 1],
+            small_send.at[k - 1],
+            small_recv.at[k - 1],
+            owners[k],
+            shard,
+        )
+
+    send_own(1, 0).start()
+    send_own(2, 1).start()
+    send_own(1, 1).start()
+    send_own(2, 0).start()
+    for k in range(1, blocks):
+        mixed_copy(k).start()
+        small_copy(k).start()
+
+    def turn(c):
+        loads[c].wait()
+
+        def tile(i, carry):
+            w, block = i // blocks, i % blocks
+            columns = pl.ds(pl.multiple_of(i * count, count), count)
+            turned[c, :, columns] = features[c, w, block].T
+            return carry
+
+        lax.fori_loop(0, seqs * blocks, tile, 0)
+
+    def grads(ref, owner):
+        place = pl.ds(pl.multiple_of(owner * lanes, lanes), lanes)
+        tall = width // 2
+
+        def tile(i, carry):
+            c, half = i // 2, i % 2
+            rows = pl.ds(pl.multiple_of(half * tall, tall), tall)
+            total = jnp.dot(
+                turned[c, rows, :],
+                ref[...].reshape(seqs * blocks * count, both),
+                preferred_element_type=jnp.float32,
+            ).astype(jnp.bfloat16)
+            out = pl.ds(pl.multiple_of(i * tall, tall), tall)
+            key_out[out, place] = total[:, :lanes]
+            value_out[out, place] = total[:, lanes:]
+            return carry
+
+        lax.fori_loop(0, 4, tile, 0)
+
+    turn(0)
+    arrived(1, 0).wait_recv()
+    pass_on(1, 0).start()
+    arrived(2, 1).wait_recv()
+    pass_on(2, 1).start()
+    turn(1)
+    grads(act_ref, p)
+    arrived(1, 1).wait_recv()
+    grads(got.at[0], beside)
+    arrived(2, 0).wait_recv()
+    grads(got.at[1], above)
+    small_out[p] = small_ref[...]
+    for k in range(1, blocks):
+        small_copy(k).wait_recv()
+        small_out[owners[k]] = small_in[k - 1]
+    mixed_out[:, :, pl.ds(pl.multiple_of(p * lanes, lanes), lanes)] = mixed_ref[p]
+    for k in range(1, blocks):
+        mixed_copy(k).wait_recv()
+        place = pl.ds(pl.multiple_of(owners[k] * lanes, lanes), lanes)
+        mixed_out[:, :, place] = mixed_in[k - 1]
+    for w in range(seqs):
+        arrived(3, w).wait_recv()
+    grads(got.at[2], across)
+    for w in range(seqs):
+        send_own(1, w).wait_send()
+        send_own(2, w).wait_send()
+        pass_on(1 + w, w).wait_send()
+    for k in range(1, blocks):
+        mixed_copy(k).wait_send()
+        small_copy(k).wait_send()
+
+
+def back(act, mixed, small, features):
+    seqs, blocks, count, both = act.shape
+    lanes = both // 2
+    width = features.shape[-1]
+    vmem = pl.BlockSpec(memory_space=pltpu.VMEM)
+    dma = pltpu.SemaphoreType.DMA
+    panel = jax.ShapeDtypeStruct((2 * width, blocks * lanes), jnp.bfloat16)
+    return pl.pallas_call(
+        back_kernel,
+        out_shape=(
+            jax.ShapeDtypeStruct((seqs, count, blocks * lanes), jnp.bfloat16),
+            panel,
+            panel,
+            jax.ShapeDtypeStruct((blocks,) + small.shape, jnp.float32),
+        ),
+        in_specs=[vmem, vmem, vmem, pl.BlockSpec(memory_space=pl.ANY)],
+        out_specs=[vmem] * 4,
+        scratch_shapes=[
+            pltpu.VMEM(features.shape, jnp.bfloat16),
+            pltpu.VMEM((2, width, seqs * blocks * count), jnp.bfloat16),
+            pltpu.VMEM((3,) + act.shape, jnp.bfloat16),
+            pltpu.VMEM((blocks - 1,) + mixed.shape[1:], jnp.bfloat16),
+            pltpu.VMEM((blocks - 1,) + small.shape, jnp.float32),
+            dma((3, seqs)),
+            dma((3, seqs)),
+            dma((blocks - 1,)),
+            dma((blocks - 1,)),
+            dma((blocks - 1,)),
+            dma((blocks - 1,)),
+            dma((2,)),
+        ],
+        compiler_params=pltpu.CompilerParams(
+            collective_id=1, has_side_effects=True, vmem_limit_bytes=48 * 1024 * 1024
+        ),
+        cost_estimate=pl.CostEstimate(
+            flops=8 * seqs * blocks * count * width * blocks * lanes,
+            bytes_accessed=4 * blocks * seqs * count * width,
+            transcendentals=0,
+        ),
+    )(act, mixed, small, features)
+
+
 def by_channels(inputs, key_panel, value_panel, short_filters, medium_filters, lengths, cotangent):
     seqs, count, width = inputs.shape
     blocks = lax.axis_size("dp")
@@ -695,26 +898,16 @@
     groups = medium_filters.shape[0] // blocks
     mine = lax.axis_index("dp")
     keys, values, cot, features = front(inputs, key_panel, value_panel, cotangent, blocks)
-    features = features.reshape(2, blocks * seqs * count, width)
     short = lax.dynamic_slice_in_dim(short_filters, mine * lanes, lanes, 1)
     medium = lax.dynamic_slice_in_dim(medium_filters, mine * groups, groups, 0)
-    mixed, key_act, value_act, short_grad, medium_grad = hyena(
-        keys, values, cot, short, medium, lengths
-    )
-
-    def panel_grad(act):
-        gathered = lax.all_gather(act.reshape(-1, lanes), "dp", axis=1, tiled=True)
-        return (
-            jnp.einsum("cnf,nm->cfm", features, gathered, preferred_element_type=jnp.float32)
-            .astype(jnp.bfloat16)
-            .reshape(2 * width, channels)
-        )
-
-    key_grad, value_grad = panel_grad(key_act), panel_grad(value_act)
-    mixed = lax.all_to_all(mixed, "dp", split_axis=0, concat_axis=2, tiled=False)
-    mixed = mixed.reshape(seqs, count, channels)
-    short_grad = lax.all_gather(short_grad, "dp", axis=1, tiled=True)
-    medium_grad = lax.all_gather(medium_grad, "dp", axis=0, tiled=True)
+    mixed, act, small = hyena(keys, values, cot, short, medium, lengths)
+    mixed, key_grad, value_grad, small = back(act, mixed, small, features)
+    taps, medium_taps = short_filters.shape[-1], medium_filters.shape[-1]
+    short_grad = small[:, :16].reshape(blocks, 2, 8, lanes)[:, :, :taps]
+    short_grad = short_grad.transpose(1, 0, 3, 2).reshape(2, channels, taps)
+    sums = small[:, 16:].reshape(blocks, 2, groups, BLOCK).transpose(0, 2, 1, 3)
+    sums = sums.reshape(blocks * groups, 2 * BLOCK)
+    medium_grad = sums[:, BLOCK - medium_taps + 1 : BLOCK + 1][:, ::-1]
     return (mixed, key_grad, value_grad, short_grad, medium_grad)
 
 

time: 264 us -> 217 us (0.82)
  Pallas kernels: 153 us -> 206 us
  waiting for transfers between devices: 41.6 us -> 0 us
  matrix products: 19.7 us -> 0 us
  blocking collectives: 19.7 us -> 0 us
  between operations: 14.1 us -> 0.71 us
  starting transfers between devices: 7.88 us -> 0 us
  local copies, waits for them, and re-layouts: 7.33 us -> 10.6 us
    pallas_call x0 -> x1, Pallas kernels: none -> 53.2 us  [back(): pl.pallas_call(back_kernel, out_shape=(jax.ShapeDtypeStruct((seqs, count,...]
    all_gather x2 -> x0, waiting for transfers between devices: 40.9 us -> none  [panel_grad(): gathered = lax.all_gather(act.reshape(-1, lanes), 'dp', axis=1, tiled=True)]
    dot_general x2 -> x0, matrix products: 19.7 us -> none  [panel_grad(): jnp.einsum('cnf,nm->cfm', features, gathered, preferred_element_type=jnp....]
    all_gather x2 -> x0, blocking collectives: 19.7 us -> none  [the longest x1 10.3 us: by_channels(): medium_grad = lax.all_gather(medium_grad, 'dp', axis=0, tiled=True)]
    all_to_all x1 -> x0, starting transfers between devices: 7.8 us -> none  [by_channels(): lax.all_to_all(mixed, 'dp', split_axis=0, concat_axis=2, tiled=False)]
    unnamed x14 -> x16, local copies, waits for them, and re-layouts: 6.11 us -> 8.33 us
  transfers between devices with their start and end apart: 3 -> 0, of which waited for: 2 -> 0; matrix products, arithmetic and copies ran while one was open for 5% -> 0% of each run, Pallas kernels for 0% -> 0%
where the time goes in v3:
time: 217 us
  Pallas kernels  206 us (95%)
  local copies, waits for them, and re-layouts  10.6 us (5%)
    pallas_call x1, Pallas kernels, front(): pl.pallas_call(front_kernel, out_shape=(acts, acts, jax.ShapeDtypeStruct(...  140 us
    pallas_call x1, Pallas kernels, back(): pl.pallas_call(back_kernel, out_shape=(jax.ShapeDtypeStruct((seqs, count,...  53.2 us
    pallas_call x1, Pallas kernels, hyena(): pl.pallas_call(functools.partial(hyena_kernel, taps, lanes // groups), ou...  12.2 us
    unnamed x16, local copies, waits for them, and re-layouts  8.33 us

profile of v3, /device:TPU:0, one launch (start us, length us, event | category | flops | bytes accessed | tf_op | source)
XLA Modules:
  0.0 217.0 jit_solution(16219892801726940362)
XLA Ops:
  0.6 0.0 copy-start
  0.7 0.7 constant_dynamic-slice_fusion
  1.3 0.1 rev.6
  1.4 0.1 pad.14.reversed_ref
  1.5 0.0 copy-done
  1.5 0.0 copy-start.1
  1.5 1.6 copy-done.1
  3.1 0.0 copy-start.2
  3.1 1.2 copy-done.2
  4.3 0.0 copy-start.3
  4.3 1.0 copy-done.3
  5.4 0.0 copy-start.4
  5.4 140.3 %shard_map.110 = (bf16[2,4,256,128]{3,2,1,0:T(8,128)(2,1)S(1)}, bf16[2,4,256,128]{3,2,1,0:T(8,128)(2,1)S(1)}, bf16[4,2,256,128]{3,2,1,0:T(8,128)(2,1)S(1)}, bf16[2,2,4,256,1024]{4,3,2,1,0:T(8,128)(2,1)}) custom-call(bf16[2,256,1024]{2,1,0:T(8,128)(2,1)S(1)} %copy-done.2, bf16[2048,512]{1,0:T(8,128)(2,1)S(1)} %copy-done.1, bf16[2048,512]{1,0:T(8,128)(2,1)} %value_ref.1, ...), custom_call_target="tpu_custom_call" | custom-call | flops 8589934592 | bytes 16777216 | tf_op jit(solution)/shard_map/pallas_call | solution.py:642
  145.7 0.0 copy-done.4
  145.7 12.2 %shard_map.111 = (bf16[4,2,256,128]{3,2,1,0:T(8,128)(2,1)S(1)}, bf16[2,4,256,256]{3,2,1,0:T(8,128)(2,1)S(1)}, f32[32,128]{1,0:T(8,128)S(1)}) custom-call(s32[2]{0:T(128)S(1)} %copy-done.4, bf16[2,4,256,128]{3,2,1,0:T(8,128)(2,1)S(1)} %get-tuple-element.16.keys_ref, bf16[2,4,256,128]{3,2,1,0:T(8,128)(2,1)S(1)} %get-tuple-element.17.values_ref, ...), custom_call_target="tpu_custom_call" | custom-call | flops 6442450944 | bytes 3145728 | tf_op jit(solution)/shard_map/pallas_call | solution.py:300
  157.9 53.2 %shard_map.112 = (bf16[2,256,512]{2,1,0:T(8,128)(2,1)S(1)}, bf16[2048,512]{1,0:T(8,128)(2,1)S(1)}, bf16[2048,512]{1,0:T(8,128)(2,1)}, f32[4,32,128]{2,1,0:T(8,128)S(1)}) custom-call(bf16[2,4,256,256]{3,2,1,0:T(8,128)(2,1)S(1)} %get-tuple-element.19.act_ref, bf16[4,2,256,128]{3,2,1,0:T(8,128)(2,1)S(1)} %get-tuple-element.20.mixed_ref, ...), custom_call_target="tpu_custom_call" | custom-call | flops 8589934592 | bytes 8388608 | tf_op jit(solution)/shard_map/pallas_call | solution.py:858
  211.1 0.1 slice.17
  211.2 0.7 rev.7
  211.9 0.6 reshape.23
  212.5 0.8 copy.20
  213.3 0.0 copy-start.5
  213.3 1.3 copy.21
  214.6 1.0 copy-done.5
  215.7 1.3 copy.22
  (7 shorter events, 0.0 us)
Async XLA Ops:
  0.6 0.9 copy-start
  1.5 1.6 copy-start.1
  3.1 1.2 copy-start.2
  4.3 1.0 copy-start.3
  5.4 140.3 %copy-start.4 = (s32[2]{0:T(128)S(1)}, s32[2]{0:T(128)}, u32[]{:S(2)}) copy-start(s32[2]{0:T(128)} %lengths_ref.1) | copy-start | bytes 28
  213.3 2.3 %copy-start.5 = (bf16[2048,512]{1,0:T(8,128)(2,1)S(1)}, bf16[2048,512]{1,0:T(8,128)(2,1)}, u32[]{:S(2)}) copy-start(bf16[2048,512]{1,0:T(8,128)(2,1)} %get-tuple-element.36) | copy-start | bytes 6291460

commit v4 on v3

--- a/solution.py
+++ b/solution.py
@@ -365,10 +365,13 @@
     cot_recv,
     local,
     saved,
+    panel_sem,
+    cot_local,
 ):
     seqs, count, width = x_ref.shape
     blocks, lanes = cot_in.shape[0], cot_in.shape[-1]
     rows = count // 2
+    chunks = 2 * seqs
     p, shard = lax.axis_index("dp"), lax.axis_index("shard")
     z, core = shard // 2, shard % 2
     sibling = z * 2 + (1 - core)
@@ -393,63 +396,54 @@
         greet(p, (shard + step) % (2 * blocks))
     pl.semaphore_wait(barrier, blocks + 2)
 
-    def part(half):
-        return pl.ds(half * rows, rows)
-
-    def held(h, layer, w, half):
-        return x_ref.at[w, part(half)] if h == 0 else line.at[layer, w, part(half)]
-
-    def line_copy(h, layer, w, half, way):
-        piece = w * 2 + half
-        return remote(
-            held(h, layer, w, half),
-            line.at[layer, w, part(half)],
-            line_send.at[way, layer, piece],
-            line_recv.at[layer, piece],
+    def block_of(k):
+        return x_ref.at[k // 2, pl.ds(k % 2 * rows, rows)]
+
+    def held(h, layer, k):
+        return block_of(k) if h == 0 else line.at[layer, k]
+
+    def line_copy(h, layer, k, way):
+        return remote(
+            held(h, layer, k),
+            line.at[layer, k],
+            line_send.at[way, layer, k],
+            line_recv.at[layer, k],
             p,
             shard + 2 * (1 - 2 * way),
         )
 
-    def plane_copy(h, layer, w, half):
-        piece = w * 2 + half
-        return remote(
-            held(h, layer, w, half),
-            features.at[core, w, p, part(half)],
-            plane_send.at[layer, piece],
-            plane_recv.at[p, piece],
+    def plane_copy(h, layer, k):
+        return remote(
+            held(h, layer, k),
+            features.at[core, k, p],
+            plane_send.at[layer, k],
+            plane_recv.at[p, k],
             layer,
             shard,
         )
 
-    def plane_arrival(block, w, half):
-        piece = w * 2 + half
-        place = features.at[core, w, block, part(half)]
-        return remote(
-            place, place, plane_send.at[block, piece], plane_recv.at[block, piece], block, shard
-        )
-
-    def core_copy(source, block, w, half):
-        piece = w * 2 + half
+    def plane_arrival(block, k):
+        place = features.at[core, k, block]
+        return remote(
+            place, place, plane_send.at[block, k], plane_recv.at[block, k], block, shard
+        )
+
+    def core_copy(source, block, k):
         return remote(
             source,
-            features.at[core, w, block, part(half)],
-            core_send.at[block, piece],
-            core_recv.at[block, piece],
+            features.at[core, k, block],
+            core_send.at[block, k],
+            core_recv.at[block, k],
             p,
             sibling,
         )
 
-    def core_arrival(block, w, half):
-        piece = w * 2 + half
-        place = features.at[1 - core, w, block, part(half)]
-        return remote(
-            place, place, core_send.at[block, piece], core_recv.at[block, piece], p, sibling
-        )
-
-    def keep_copy(h, layer, w, half):
-        return pltpu.make_async_copy(
-            held(h, layer, w, half), features.at[core, w, p, part(half)], local.at[w * 2 + half]
-        )
+    def core_arrival(block, k):
+        place = features.at[1 - core, k, block]
+        return remote(place, place, core_send.at[block, k], core_recv.at[block, k], p, sibling)
+
+    def keep_copy(h, layer, k):
+        return pltpu.make_async_copy(held(h, layer, k), features.at[core, k, p], local.at[k])
 
     def steps(h):
         if h == 0:
@@ -459,87 +453,87 @@
             (1, z + h, z + h < blocks, z > 0),
         ]
 
-    def dispatch(h, layer, w, half):
+    def dispatch(h, layer, k):
         @pl.when(layer == p)
         def _():
-            keep_copy(h, layer, w, half).start()
-            core_copy(held(h, layer, w, half), p, w, half).start()
+            keep_copy(h, layer, k).start()
+            core_copy(held(h, layer, k), p, k).start()
 
         @pl.when(layer != p)
         def _():
-            plane_copy(h, layer, w, half).start()
-
-    def hop(w, h):
-        for half in range(2):
-            if h == 0:
-                for way, layer, _, onward in steps(0):
-
-                    @pl.when(onward)
-                    def _():
-                        line_copy(0, layer, w, half, way).start()
-
-                dispatch(0, z, w, half)
-            else:
-                for way, layer, valid, onward in steps(h):
-
-                    @pl.when(valid)
-                    def _():
-                        line_copy(h, layer, w, half, way).wait_recv()
-
-                        @pl.when(onward)
-                        def _():
-                            line_copy(h, layer, w, half, way).start()
-
-                        dispatch(h, layer, w, half)
-
-    def share(w):
-        for half in range(2):
-            for j in range(1, blocks):
-                plane_arrival(froms[j], w, half).wait_recv()
-                place = features.at[core, w, froms[j], part(half)]
-                core_copy(place, froms[j], w, half).start()
-
-    def save_copy(w):
-        return pltpu.make_async_copy(features.at[:, w], features_out.at[:, w], saved.at[w])
-
-    def complete(w):
-        for half in range(2):
-            for j in range(blocks):
-                core_arrival(froms[j], w, half).wait_recv()
-            keep_copy(0, z, w, half).wait()
-        save_copy(w).start()
-
-    def sum_copy(w, j):
-        return remote(
-            outgoing.at[w, j - 1],
-            incoming.at[w, j - 1],
-            sum_send.at[w, j - 1],
-            sum_recv.at[w, j - 1],
-            peers[j],
+            plane_copy(h, layer, k).start()
+
+    def hop(k, h):
+        if h == 0:
+            for way, layer, _, onward in steps(0):
+
+                @pl.when(onward)
+                def _():
+                    line_copy(0, layer, k, way).start()
+
+            dispatch(0, z, k)
+            return
+        for way, layer, valid, onward in steps(h):
+
+            @pl.when(valid)
+            def _():
+                line_copy(h, layer, k, way).wait_recv()
+
+                @pl.when(onward)
+                def _():
+                    line_copy(h, layer, k, way).start()
+
+                dispatch(h, layer, k)
+
+    def share(k):
+        for j in range(1, blocks):
+            plane_arrival(froms[j], k).wait_recv()
+            core_copy(features.at[core, k, froms[j]], froms[j], k).start()
+
+    def save_copy(k):
+        return pltpu.make_async_copy(features.at[:, k], features_out.at[:, k], saved.at[k])
+
+    def complete(k):
+        for j in range(blocks):
+            core_arrival(froms[j], k).wait_recv()
+        keep_copy(0, z, k).wait()
+        save_copy(k).start()
+
+    def sum_copy(k, j):
+        return remote(
+            outgoing.at[k, j - 1],
+            incoming.at[k, j - 1],
+            sum_send.at[k, j - 1],
+            sum_recv.at[k, j - 1],
+            (p + j) % blocks,
             shard,
         )
 
-    def project(w, j):
-        def tile(i, carry):
-            total = jnp.zeros((count, 2 * lanes), jnp.float32)
-            for c in range(2):
-                total += jnp.dot(
-                    features[c, w, i], panels[peers[j], c], preferred_element_type=jnp.float32
-                )
-            if j == 0:
-                own[w, i] = total
-            else:
-                outgoing[w, j - 1, i] = total.astype(jnp.bfloat16)
+    def product(k, owner):
+        total = jnp.zeros((blocks * rows, 2 * lanes), jnp.float32)
+        for c in range(2):
+            total += jnp.dot(
+                features[c, k].reshape(blocks * rows, width),
+                panels[owner, c],
+                preferred_element_type=jnp.float32,
+            )
+        return total
+
+    def project(k):
+        def others(j, carry):
+            outgoing[k, j - 1] = product(k, (p + j) % blocks).astype(jnp.bfloat16)
+            sum_copy(k, j).start()
             return carry
 
-        lax.fori_loop(0, blocks, tile, 0)
-        if j > 0:
-            sum_copy(w, j).start()
+        lax.fori_loop(1, blocks, others, 0)
+        own[k] = product(k, p)
+
+    def cot_place(owner):
+        return pl.ds(pl.multiple_of(owner * lanes, lanes), lanes)
 
     def cot_copy(j):
-        place = pl.ds(pl.multiple_of(peers[j] * lanes, lanes), lanes)
-        return remote(
-            cot_ref.at[:, :, place],
+        return remote(
+            cot_ref.at[:, :, cot_place(peers[j])],
             cot_in.at[p],
             cot_send.at[j],
             cot_recv.at[p],
@@ -548,82 +542,86 @@
         )
 
     def cot_arrival(j):
-        return remote(
-            cot_in.at[froms[j]],
-            cot_in.at[froms[j]],
-            cot_send.at[j],
-            cot_recv.at[froms[j]],
-            froms[j],
-            shard,
-        )
+        place = cot_in.at[froms[j]]
+        return remote(place, place, cot_send.at[j], cot_recv.at[froms[j]], froms[j], shard)
+
+    cot_keep = pltpu.make_async_copy(
+        cot_ref.at[:, :, cot_place(p)], cot_in.at[p], cot_local.at[0]
+    )
+    panel_copies = [
+        pltpu.make_async_copy(
+            ref.at[pl.ds(c * width, width), pl.ds(r * lanes, lanes)],
+            panels.at[r, c, :, pl.ds(branch * lanes, lanes)],
+            panel_sem.at[branch, r, c],
+        )
+        for branch, ref in ((0, key_ref), (1, value_ref))
+        for r in range(blocks)
+        for c in range(2)
+    ]
 
     hop(0, 0)
-    for r in range(blocks):
-        for c in range(2):
-            source = pl.ds(c * width, width)
-            columns = slice(r * lanes, (r + 1) * lanes)
-            panels[r, c, :, 0:lanes] = key_ref[source, columns]
-            panels[r, c, :, lanes : 2 * lanes] = value_ref[source, columns]
-    for h in range(1, blocks):
-        hop(0, h)
-    hop(1, 0)
-    share(0)
-    hop(1, 1)
-    complete(0)
-    project(0, 2)
-    project(0, 1)
-    hop(1, 2)
-    project(0, 3)
-    hop(1, 3)
-    project(0, 0)
-    share(1)
     for j in range(1, blocks):
         cot_copy(j).start()
-    cot_in[p] = cot_ref[:, :, pl.ds(pl.multiple_of(p * lanes, lanes), lanes)]
-    complete(1)
-    for j in (1, 3, 2, 0):
-        project(1, j)
+    cot_keep.start()
+    for copy in panel_copies:
+        copy.start()
+    hop(0, 1)
+    hop(0, 2)
+    hop(1, 0)
+    hop(0, 3)
+    for k in range(1, chunks):
+        hop(k, 1)
+        hop(k, 2)
+        if k + 1 < chunks:
+            hop(k + 1, 0)
+        share(k - 1)
+        hop(k, 3)
+        complete(k - 1)
+        if k == 1:
+            for copy in panel_copies:
+                copy.wait()
+        project(k - 1)
+    share(chunks - 1)
+    cot_keep.wait()
     for j in range(1, blocks):
         cot_arrival(j).wait_recv()
     cot_out[...] = cot_in[...]
-    for w in range(seqs):
+    complete(chunks - 1)
+    project(chunks - 1)
+    for k in range(chunks):
         for j in range(1, blocks):
-            sum_copy(w, j).wait_recv()
-
-        def add(i, carry):
-            total = own[w, i]
-            for j in range(1, blocks):
-                total += incoming[w, j - 1, i].astype(jnp.float32)
-            keys_ref[w, i] = total[:, 0:lanes].astype(jnp.bfloat16)
-            values_ref[w, i] = total[:, lanes : 2 * lanes].astype(jnp.bfloat16)
-            return carry
-
-        lax.fori_loop(0, blocks, add, 0)
-
-    for w in range(seqs):
-        save_copy(w).wait()
+            sum_copy(k, j).wait_recv()
+        total = own[k]
         for j in range(1, blocks):
-            sum_copy(w, j).wait_send()
-        for half in range(2):
-            for j in range(blocks):
-                core_copy(features.at[core, w, froms[j], part(half)], froms[j], w, half).wait_send()
-            for h in range(blocks):
-                for way, layer, valid, onward in steps(h):
+            total += incoming[k, j - 1].astype(jnp.float32)
+        total = total.astype(jnp.bfloat16).reshape(blocks, rows, 2 * lanes)
+        place = pl.ds(k % 2 * rows, rows)
+        keys_ref[k // 2, :, place, :] = total[:, :, 0:lanes]
+        values_ref[k // 2, :, place, :] = total[:, :, lanes : 2 * lanes]
+
+    for k in range(chunks):
+        save_copy(k).wait()
+        for j in range(1, blocks):
+            sum_copy(k, j).wait_send()
+        for j in range(blocks):
+            core_copy(features.at[core, k, froms[j]], froms[j], k).wait_send()
+        for h in range(blocks):
+            for way, layer, valid, onward in steps(h):
+                if h > 0:
+                    onward = jnp.logical_and(valid, onward)
+
+                @pl.when(onward)
+                def _():
+                    line_copy(h, layer, k, way).wait_send()
+
+                if h > 0 or way == 0:
+                    sent = layer != p
                     if h > 0:
-                        onward = jnp.logical_and(valid, onward)
-
-                    @pl.when(onward)
+                        sent = jnp.logical_and(valid, sent)
+
+                    @pl.when(sent)
                     def _():
-                        line_copy(h, layer, w, half, way).wait_send()
-
-                    if h > 0 or way == 0:
-                        sent = layer != p
-                        if h > 0:
-                            sent = jnp.logical_and(valid, sent)
-
-                        @pl.when(sent)
-                        def _():
-                            plane_copy(h, layer, w, half).wait_send()
+                        plane_copy(h, layer, k).wait_send()
 
     for j in range(1, blocks):
         cot_copy(j).wait_send()
@@ -637,7 +635,8 @@
     vmem = pl.BlockSpec(memory_space=pltpu.VMEM)
     hbm = pl.BlockSpec(memory_space=pl.ANY)
     acts = jax.ShapeDtypeStruct((seqs, blocks, count, lanes), jnp.bfloat16)
-    feature_shape = (2, seqs, blocks, count, width)
+    feature_shape = (2, pieces, blocks, count // 2, width)
+    tall = blocks * count // 2
     dma = pltpu.SemaphoreType.DMA
     return pl.pallas_call(
         front_kernel,
@@ -647,15 +646,15 @@
             jax.ShapeDtypeStruct((blocks, seqs, count, lanes), jnp.bfloat16),
             jax.ShapeDtypeStruct(feature_shape, jnp.bfloat16),
         ),
-        in_specs=[hbm, vmem, vmem, vmem],
+        in_specs=[hbm] * 4,
         out_specs=[vmem, vmem, vmem, hbm],
         scratch_shapes=[
-            pltpu.VMEM((blocks, seqs, count, width), jnp.bfloat16),
+            pltpu.VMEM((blocks, pieces, count // 2, width), jnp.bfloat16),
             pltpu.VMEM(feature_shape, jnp.bfloat16),
             pltpu.VMEM((blocks, 2, width, 2 * lanes), jnp.bfloat16),
-            pltpu.VMEM((seqs, blocks, count, 2 * lanes), jnp.float32),
-            pltpu.VMEM((seqs, blocks - 1, blocks, count, 2 * lanes), jnp.bfloat16),
-            pltpu.VMEM((seqs, blocks - 1, blocks, count, 2 * lanes), jnp.bfloat16),
+            pltpu.VMEM((pieces, tall, 2 * lanes), jnp.float32),
+            pltpu.VMEM((pieces, blocks - 1, tall, 2 * lanes), jnp.bfloat16),
+            pltpu.VMEM((pieces, blocks - 1, tall, 2 * lanes), jnp.bfloat16),
             pltpu.VMEM((blocks, seqs, count, lanes), jnp.bfloat16),
             dma((2, blocks, pieces)),
             dma((blocks, pieces)),
@@ -663,12 +662,14 @@
             dma((blocks, pieces)),
             dma((blocks, pieces)),
             dma((blocks, pieces)),
-            dma((seqs, blocks - 1)),
-            dma((seqs, blocks - 1)),
+            dma((pieces, blocks - 1)),
+            dma((pieces, blocks - 1)),
             dma((blocks,)),
             dma((blocks,)),
             dma((pieces,)),
-            dma((seqs,)),
+            dma((pieces,)),
+            dma((2, blocks, 2)),
+            dma((1,)),
         ],
         compiler_params=pltpu.CompilerParams(
             collective_id=0, has_side_effects=True, vmem_limit_bytes=48 * 1024 * 1024
@@ -790,12 +791,14 @@
         loads[c].wait()
 
         def tile(i, carry):
-            w, block = i // blocks, i % blocks
-            columns = pl.ds(pl.multiple_of(i * count, count), count)
-            turned[c, :, columns] = features[c, w, block].T
+            k, block = i // blocks, i % blocks
+            rows = count // 2
+            begin = ((k // 2 * blocks + block) * 2 + k % 2) * rows
+            columns = pl.ds(pl.multiple_of(begin, rows), rows)
+            turned[c, :, columns] = features[c, k, block].T
             return carry
 
-        lax.fori_loop(0, seqs * blocks, tile, 0)
+        lax.fori_loop(0, 2 * seqs * blocks, tile, 0)
 
     def grads(ref, owner):
         place = pl.ds(pl.multiple_of(owner * lanes, lanes), lanes)

time: 217 us -> 193 us (0.89)
  Pallas kernels: 206 us -> 182 us
    pallas_call x1, Pallas kernels: 140 us -> 119 us  [front(): pl.pallas_call(front_kernel, out_shape=(acts, acts, jax.ShapeDtypeStruct(...]
    pallas_call x1, Pallas kernels: 53.2 us -> 50.2 us  [back(): pl.pallas_call(back_kernel, out_shape=(jax.ShapeDtypeStruct((seqs, count,...]
where the time goes in v4:
time: 193 us
  Pallas kernels  182 us (94%)
  local copies, waits for them, and re-layouts  10.6 us (5%)
    pallas_call x1, Pallas kernels, front(): pl.pallas_call(front_kernel, out_shape=(acts, acts, jax.ShapeDtypeStruct(...  119 us
    pallas_call x1, Pallas kernels, back(): pl.pallas_call(back_kernel, out_shape=(jax.ShapeDtypeStruct((seqs, count,...  50.2 us
    pallas_call x1, Pallas kernels, hyena(): pl.pallas_call(functools.partial(hyena_kernel, taps, lanes // groups), ou...  12.2 us
    unnamed x16, local copies, waits for them, and re-layouts  8.33 us

profile of v4, /device:TPU:0, one launch (start us, length us, event | category | flops | bytes accessed | tf_op | source)
XLA Modules:
  0.0 192.8 jit_solution(14664369488729652106)
XLA Ops:
  0.6 0.0 copy-start
  0.7 0.7 constant_dynamic-slice_fusion
  1.3 0.1 rev.6
  1.4 0.1 pad.14.reversed_ref
  1.5 0.0 copy-done
  1.5 0.0 copy-start.1
  1.5 1.6 copy-done.1
  3.1 0.0 copy-start.2
  3.1 1.2 copy-done.2
  4.3 0.0 copy-start.3
  4.3 1.0 copy-done.3
  5.4 0.0 copy-start.4
  5.4 119.1 %shard_map.110 = (bf16[2,4,256,128]{3,2,1,0:T(8,128)(2,1)S(1)}, bf16[2,4,256,128]{3,2,1,0:T(8,128)(2,1)S(1)}, bf16[4,2,256,128]{3,2,1,0:T(8,128)(2,1)S(1)}, bf16[2,4,4,128,1024]{4,3,2,1,0:T(8,128)(2,1)}) custom-call(bf16[2,256,1024]{2,1,0:T(8,128)(2,1)S(1)} %copy-done.2, bf16[2048,512]{1,0:T(8,128)(2,1)S(1)} %copy-done.1, bf16[2048,512]{1,0:T(8,128)(2,1)} %value_ref.1, ...), custom_call_target="tpu_custom_call" | custom-call | flops 8589934592 | bytes 16777216 | tf_op jit(solution)/shard_map/pallas_call | solution.py:641
  124.5 0.0 copy-done.4
  124.5 12.2 %shard_map.111 = (bf16[4,2,256,128]{3,2,1,0:T(8,128)(2,1)S(1)}, bf16[2,4,256,256]{3,2,1,0:T(8,128)(2,1)S(1)}, f32[32,128]{1,0:T(8,128)S(1)}) custom-call(s32[2]{0:T(128)S(1)} %copy-done.4, bf16[2,4,256,128]{3,2,1,0:T(8,128)(2,1)S(1)} %get-tuple-element.16.keys_ref, bf16[2,4,256,128]{3,2,1,0:T(8,128)(2,1)S(1)} %get-tuple-element.17.values_ref, ...), custom_call_target="tpu_custom_call" | custom-call | flops 6442450944 | bytes 3145728 | tf_op jit(solution)/shard_map/pallas_call | solution.py:300
  136.7 50.2 %shard_map.112 = (bf16[2,256,512]{2,1,0:T(8,128)(2,1)S(1)}, bf16[2048,512]{1,0:T(8,128)(2,1)S(1)}, bf16[2048,512]{1,0:T(8,128)(2,1)}, f32[4,32,128]{2,1,0:T(8,128)S(1)}) custom-call(bf16[2,4,256,256]{3,2,1,0:T(8,128)(2,1)S(1)} %get-tuple-element.19.act_ref, bf16[4,2,256,128]{3,2,1,0:T(8,128)(2,1)S(1)} %get-tuple-element.20.mixed_ref, ...), custom_call_target="tpu_custom_call" | custom-call | flops 8589934592 | bytes 8388608 | tf_op jit(solution)/shard_map/pallas_call | solution.py:861
  186.9 0.1 slice.17
  187.0 0.7 rev.7
  187.7 0.6 reshape.23
  188.4 0.8 copy.20
  189.1 0.0 copy-start.5
  189.1 1.3 copy.21
  190.5 1.0 copy-done.5
  191.5 1.3 copy.22
  (7 shorter events, 0.0 us)
Async XLA Ops:
  0.6 0.9 copy-start
  1.5 1.6 copy-start.1
  3.1 1.2 copy-start.2
  4.3 1.0 copy-start.3
  5.4 119.2 %copy-start.4 = (s32[2]{0:T(128)S(1)}, s32[2]{0:T(128)}, u32[]{:S(2)}) copy-start(s32[2]{0:T(128)} %lengths_ref.1) | copy-start | bytes 28
  189.1 2.3 %copy-start.5 = (bf16[2048,512]{1,0:T(8,128)(2,1)S(1)}, bf16[2048,512]{1,0:T(8,128)(2,1)}, u32[]{:S(2)}) copy-start(bf16[2048,512]{1,0:T(8,128)(2,1)} %get-tuple-element.36) | copy-start | bytes 6291460

commit v5 on v4

v5 whole, which is shorter than its diff:
```python
import functools

import jax
import jax.numpy as jnp
from jax import lax
from jax.experimental import pallas as pl
from jax.experimental.pallas import tpu as pltpu
from jax.sharding import PartitionSpec as P

BLOCK = 128


def shifted(value, axis, steps):
    count = lax.axis_size(axis)
    first, last = (max(0, -steps), min(count, count - steps))
    return lax.ppermute(value, axis, [(source, source + steps) for source in range(first, last)])


def band(filters, count):
    groups, taps = filters.shape
    width = count + taps - 1
    padded = jnp.concatenate([filters, jnp.zeros((groups, count), jnp.float32)], axis=1)
    tiled = jnp.tile(padded, (1, count))[:, : count * width]
    return tiled.reshape(groups, count, width)


def band_sums(correlation, count, taps):
    groups, _, width = correlation.shape
    flat = correlation.reshape(groups, count * width)
    padded = jnp.concatenate([flat, jnp.zeros((groups, count), jnp.float32)], axis=1)
    skewed = padded.reshape(groups, count, width + 1)
    return jnp.sum(skewed, axis=1)[:, :taps][:, ::-1]


def short_taps(extended, filters, count):
    width = filters.shape[-1]
    total = jnp.zeros(extended.shape[:2] + (count, extended.shape[3]), jnp.float32)
    for tap in range(width):
        begin = width - 1 - tap
        total = total + filters[:, None, None, :, tap] * extended[
            :, :, begin : begin + count
        ].astype(jnp.float32)
    return total


def short_ahead(extended, filters, count):
    width = filters.shape[-1]
    total = jnp.zeros(extended.shape[:2] + (count, extended.shape[3]), jnp.float32)
    for tap in range(width):
        total = total + filters[:, None, None, :, tap] * extended[:, :, tap : tap + count]
    return total


def filter_terms(grads, extended, count, width):
    columns = []
    for tap in range(width):
        begin = width - 1 - tap
        columns.append(
            jnp.sum(grads * extended[:, :, begin : begin + count].astype(jnp.float32), axis=(1, 2))
        )
    return jnp.stack(columns, axis=-1)


def by_positions(inputs, key_panel, value_panel, short_filters, medium_filters, lengths, cotangent):
    seqs, count, local_width = inputs.shape
    channels = key_panel.shape[1]
    groups, taps = medium_filters.shape
    group_size = channels // groups
    short_width = short_filters.shape[-1]
    span = count + taps - 1
    gathered = (
        lax.all_gather(key_panel, "dp", axis=0, tiled=True),
        lax.all_gather(value_panel, "dp", axis=0, tiled=True),
    )
    panels = jnp.concatenate([gathered[0], gathered[1]], axis=1)
    features = lax.all_gather(inputs, "shard", axis=2, tiled=True)
    projected = jnp.dot(
        features.reshape(seqs * count, -1), panels, preferred_element_type=jnp.float32
    )
    paired = projected.astype(jnp.bfloat16).reshape(seqs, count, 2, channels).transpose(2, 0, 1, 3)
    head_rows = shifted(paired[:, :, count - (short_width - 1) :], "dp", 1)
    extended = jnp.concatenate([head_rows, paired], axis=2)
    smoothed = short_taps(extended, short_filters, count)
    product = (smoothed[0] * smoothed[1]).astype(jnp.bfloat16)
    before = shifted(product[:, count - (taps - 1) :], "dp", 1)
    product_ext = jnp.concatenate([before, product], axis=1).reshape(seqs, span, groups, group_size)
    forward_band = band(medium_filters[:, ::-1], count)
    response = jnp.einsum(
        "gtr,srgm->stgm",
        forward_band,
        product_ext.astype(jnp.float32),
        precision=lax.Precision.HIGHEST,
    ).reshape(seqs, count, channels)
    position = lax.axis_index("dp") * count + jnp.arange(count, dtype=jnp.int32)
    live = (position[None, :] < lengths[:, None])[:, :, None]
    mixed = jnp.where(live, response, 0.0).astype(jnp.bfloat16)
    upstream = jnp.where(live, cotangent, jnp.zeros_like(cotangent))
    after = shifted(upstream[:, : taps - 1], "dp", -1)
    upstream_ext = jnp.concatenate([upstream, after], axis=1).reshape(
        seqs, span, groups, group_size
    )
    backward_band = band(medium_filters, count)
    product_grad = jnp.einsum(
        "gtr,srgm->stgm",
        backward_band,
        upstream_ext.astype(jnp.float32),
        precision=lax.Precision.HIGHEST,
    ).reshape(seqs, count, channels)
    correlation = jnp.einsum(
        "stgm,srgm->gtr",
        upstream.reshape(seqs, count, groups, group_size),
        product_ext,
        preferred_element_type=jnp.float32,
    )
    medium_local = band_sums(correlation, count, taps)
    smooth_grad = jnp.stack([product_grad * smoothed[1], product_grad * smoothed[0]])
    short_local = filter_terms(smooth_grad, extended, count, short_width)
    ahead_rows = shifted(smooth_grad[:, :, : short_width - 1], "dp", -1)
    pair_grad = short_ahead(
        jnp.concatenate([smooth_grad, ahead_rows], axis=2), short_filters, count
    )
    short_grad, medium_grad = lax.psum((short_local, medium_local), "dp")
    outgoing = (
        pair_grad.astype(jnp.bfloat16).transpose(1, 2, 0, 3).reshape(seqs * count, 2 * channels)
    )
    flat_features = features.reshape(seqs * count, -1)
    grads = lax.psum_scatter(
        lax.dot_general(
            flat_features, outgoing, (((0,), (0,)), ((), ())), preferred_element_type=jnp.float32
        ).astype(jnp.bfloat16),
        "dp",
        scatter_dimension=0,
        tiled=True,
    ).astype(jnp.float32)
    key_grad = grads[:, :channels].astype(jnp.bfloat16)
    value_grad = grads[:, channels:].astype(jnp.bfloat16)
    return (mixed, key_grad, value_grad, short_grad, medium_grad)


def filters(
    taps,
    group,
    lengths_ref,
    keys_ref,
    values_ref,
    cot_ref,
    short_ref,
    medium_ref,
    reversed_ref,
    mixed_ref,
    act_ref,
    small_ref,
    pad_ref,
    smooth_ref,
    grad_ref,
    product_ref,
    upstream_ref,
    ahead_band,
    behind_band,
    corr_ref,
    short_acc,
):
    seqs, blocks, count, lanes = keys_ref.shape
    halves = count // BLOCK
    steps = blocks * halves
    length = blocks * count
    groups = lanes // group

    def setup():
        for g in range(groups):
            rows = pl.ds(g * BLOCK, BLOCK)
            base = jnp.broadcast_to(reversed_ref[g : g + 1, :], (BLOCK, 2 * BLOCK))
            behind_band[rows, :] = pltpu.roll(base, 0, 1, stride=1, stride_axis=0).astype(jnp.bfloat16)
            base = jnp.broadcast_to(medium_ref[g : g + 1, :], (BLOCK, 2 * BLOCK))
            ahead_band[rows, :] = pltpu.roll(base, 0, 1, stride=1, stride_axis=0).astype(jnp.bfloat16)

        zeros8 = jnp.zeros((8, lanes), jnp.float32)
        zeros_block = jnp.zeros((BLOCK, lanes), jnp.bfloat16)
        for s in range(seqs):
            for branch in range(2):
                pad_ref[branch, s, pl.ds(0, 8), :] = zeros8
                grad_ref[branch, s, pl.ds(length, 8), :] = zeros8
            product_ref[pl.ds(0, BLOCK), pl.ds(s * lanes, lanes)] = zeros_block
            upstream_ref[pl.ds(length, BLOCK), pl.ds(s * lanes, lanes)] = zeros_block

        corr_ref[...] = jnp.zeros_like(corr_ref)
        short_acc[...] = jnp.zeros_like(short_acc)

    def window(s):
        lane_place = pl.ds(s * lanes, lanes)
        lane_group = lax.broadcasted_iota(jnp.int32, (BLOCK, lanes), 1) // group

        def smooth(step, carry):
            block, half = step // halves, step % halves
            source = pl.ds(pl.multiple_of(half * BLOCK, BLOCK), BLOCK)
            begin = pl.multiple_of(step * BLOCK, BLOCK)
            place = lax.broadcasted_iota(jnp.int32, (BLOCK, lanes), 0) + begin
            parts = []
            for branch, ref in ((0, keys_ref), (1, values_ref)):
                now = ref[s, block, source, :].astype(jnp.float32)
                pad_ref[branch, s, pl.ds(begin + 8, BLOCK), :] = now
                window = pad_ref[branch, s, pl.ds(begin, BLOCK + 8), :]
                total = short_ref[branch, 0:1, :] * now
                for tap in range(1, taps):
                    total += short_ref[branch, tap : tap + 1, :] * window[8 - tap : 8 - tap + BLOCK]
                smooth_ref[branch, s, pl.ds(begin, BLOCK), :] = total
                parts.append(total)
            columns = pl.ds(s * lanes, lanes)
            product_ref[pl.ds(begin + BLOCK, BLOCK), columns] = (parts[0] * parts[1]).astype(
                jnp.bfloat16
            )
            cot = cot_ref[block, s, source, :].astype(jnp.float32)
            upstream_ref[pl.ds(begin, BLOCK), columns] = jnp.where(
                place < lengths_ref[s], cot, 0.0
            ).astype(jnp.bfloat16)
            return carry

        lax.fori_loop(0, steps, smooth, 0)


        def own(stacked):
            chosen = stacked[0:BLOCK]
            for g in range(1, groups):
                chosen = jnp.where(lane_group == g, stacked[g * BLOCK : (g + 1) * BLOCK], chosen)
            return chosen

        def mix(step, carry):
            block, half = step // halves, step % halves
            source = pl.ds(pl.multiple_of(half * BLOCK, BLOCK), BLOCK)
            begin = pl.multiple_of(step * BLOCK, BLOCK)
            place = lax.broadcasted_iota(jnp.int32, (BLOCK, lanes), 0) + begin
            past = product_ref[pl.ds(begin, 2 * BLOCK), lane_place]
            response = own(jnp.dot(behind_band[...], past, preferred_element_type=jnp.float32))
            future = upstream_ref[pl.ds(begin, 2 * BLOCK), lane_place]
            product_grad = own(jnp.dot(ahead_band[...], future, preferred_element_type=jnp.float32))
            here = future[0:BLOCK]
            apart = jnp.concatenate(
                [jnp.where(lane_group == g, here, jnp.zeros_like(here)) for g in range(groups)], axis=0
            )
            corr_ref[...] += lax.dot_general(
                apart, past, (((1,), (1,)), ((), ())), preferred_element_type=jnp.float32
            )
            mixed_ref[block, s, source, :] = jnp.where(
                place < lengths_ref[s], response, 0.0
            ).astype(jnp.bfloat16)
            for branch in range(2):
                grad = product_grad * smooth_ref[1 - branch, s, pl.ds(begin, BLOCK), :]
                grad_ref[branch, s, pl.ds(begin, BLOCK), :] = grad
                window = pad_ref[branch, s, pl.ds(begin, BLOCK + 8), :]
                for tap in range(taps):
                    term = grad * window[8 - tap : 8 - tap + BLOCK]
                    short_acc[branch, tap] += jnp.sum(term.reshape(BLOCK // 8, 8, lanes), axis=0)
            return carry

        lax.fori_loop(0, steps, mix, 0)

        def back(step, carry):
            block, half = step // halves, step % halves
            source = pl.ds(pl.multiple_of(half * BLOCK, BLOCK), BLOCK)
            begin = pl.multiple_of(step * BLOCK, BLOCK)
            for branch in range(2):
                window = grad_ref[branch, s, pl.ds(begin, BLOCK + 8), :]
                total = short_ref[branch, 0:1, :] * window[0:BLOCK]
                for tap in range(1, taps):
                    total += short_ref[branch, tap : tap + 1, :] * window[tap : tap + BLOCK]
                columns = slice(branch * lanes, (branch + 1) * lanes)
                act_ref[s, block, source, columns] = total.astype(jnp.bfloat16)
            return carry

        lax.fori_loop(0, steps, back, 0)


    def finish():
        for branch in range(2):
            for tap in range(8):
                if tap < taps:
                    sums = jnp.sum(short_acc[branch, tap], axis=0, keepdims=True)
                else:
                    sums = jnp.zeros((1, lanes), jnp.float32)
                small_ref[branch * 8 + tap : branch * 8 + tap + 1, :] = sums
        for g in range(groups):
            rows = BLOCK
            total = corr_ref[pl.ds(g * BLOCK, BLOCK), :]
            while rows > 1:
                rows //= 2
                total = total[:rows] + pltpu.roll(total[rows:], 2 * BLOCK - rows, 1)
            small_ref[16 + g : 17 + g, :] = total[:, :BLOCK]
            small_ref[16 + groups + g : 17 + groups + g, :] = total[:, BLOCK:]

    return setup, window, finish


def remote(source, target, send, recv, dp, shard):
    return pltpu.make_async_remote_copy(
        src_ref=source,
        dst_ref=target,
        send_sem=send,
        recv_sem=recv,
        device_id={"dp": dp, "shard": shard},
        device_id_type=pl.DeviceIdType.MESH,
    )


def front(
    x_ref,
    key_ref,
    value_ref,
    cot_ref,
    keys_ref,
    values_ref,
    line,
    features,
    panels,
    own,
    outgoing,
    incoming,
    cot_in,
    line_send,
    line_recv,
    plane_send,
    plane_recv,
    core_send,
    core_recv,
    sum_send,
    sum_recv,
    cot_send,
    cot_recv,
    local,
    panel_sem,
    cot_local,
):
    seqs, count, width = x_ref.shape
    blocks, lanes = cot_in.shape[0], cot_in.shape[-1]
    rows = count // 2
    chunks = 2 * seqs
    p, shard = lax.axis_index("dp"), lax.axis_index("shard")
    z, core = shard // 2, shard % 2
    sibling = z * 2 + (1 - core)
    peers = [(p + j) % blocks for j in range(blocks)]
    froms = [(p + blocks - j) % blocks for j in range(blocks)]

    barrier = pltpu.get_barrier_semaphore()

    def greet(dp, to):
        pl.semaphore_signal(
            barrier,
            inc=1,
            device_id={"dp": dp, "shard": to},
            device_id_type=pl.DeviceIdType.MESH,
        )

    greet(p, sibling)
    for j in range(1, blocks):
        greet(peers[j], shard)

    for step in (2, 2 * blocks - 2):
        greet(p, (shard + step) % (2 * blocks))
    pl.semaphore_wait(barrier, blocks + 2)

    def block_of(k):
        return x_ref.at[k // 2, pl.ds(k % 2 * rows, rows)]

    def held(h, layer, k):
        return block_of(k) if h == 0 else line.at[layer, k]

    def line_copy(h, layer, k, way):
        return remote(
            held(h, layer, k),
            line.at[layer, k],
            line_send.at[way, layer, k],
            line_recv.at[layer, k],
            p,
            shard + 2 * (1 - 2 * way),
        )

    def plane_copy(h, layer, k):
        return remote(
            held(h, layer, k),
            features.at[core, k, p],
            plane_send.at[layer, k],
            plane_recv.at[p, k],
            layer,
            shard,
        )

    def plane_arrival(block, k):
        place = features.at[core, k, block]
        return remote(
            place, place, plane_send.at[block, k], plane_recv.at[block, k], block, shard
        )

    def core_copy(source, block, k):
        return remote(
            source,
            features.at[core, k, block],
            core_send.at[block, k],
            core_recv.at[block, k],
            p,
            sibling,
        )

    def core_arrival(block, k):
        place = features.at[1 - core, k, block]
        return remote(place, place, core_send.at[block, k], core_recv.at[block, k], p, sibling)

    def keep_copy(h, layer, k):
        return pltpu.make_async_copy(held(h, layer, k), features.at[core, k, p], local.at[k])

    def steps(h):
        if h == 0:
            return [(0, z, None, z < blocks - 1), (1, z, None, z > 0)]
        return [
            (0, z - h, z - h >= 0, z < blocks - 1),
            (1, z + h, z + h < blocks, z > 0),
        ]

    def dispatch(h, layer, k):
        @pl.when(layer == p)
        def _():
            keep_copy(h, layer, k).start()
            core_copy(held(h, layer, k), p, k).start()

        @pl.when(layer != p)
        def _():
            plane_copy(h, layer, k).start()

    def hop(k, h):
        if h == 0:
            for way, layer, _, onward in steps(0):

                @pl.when(onward)
                def _():
                    line_copy(0, layer, k, way).start()

            dispatch(0, z, k)
            return
        for way, layer, valid, onward in steps(h):

            @pl.when(valid)
            def _():
                line_copy(h, layer, k, way).wait_recv()

                @pl.when(onward)
                def _():
                    line_copy(h, layer, k, way).start()

                dispatch(h, layer, k)

    def share(k):
        for j in range(1, blocks):
            plane_arrival(froms[j], k).wait_recv()
            core_copy(features.at[core, k, froms[j]], froms[j], k).start()

    def complete(k):
        for j in range(blocks):
            core_arrival(froms[j], k).wait_recv()
        keep_copy(0, z, k).wait()

    def sum_copy(k, j):
        return remote(
            outgoing.at[k, j - 1],
            incoming.at[k, j - 1],
            sum_send.at[k, j - 1],
            sum_recv.at[k, j - 1],
            (p + j) % blocks,
            shard,
        )

    def product(k, owner):
        total = jnp.zeros((blocks * rows, 2 * lanes), jnp.float32)
        for c in range(2):
            total += jnp.dot(
                features[c, k].reshape(blocks * rows, width),
                panels[owner, c],
                preferred_element_type=jnp.float32,
            )
        return total

    def project(k):
        def others(j, carry):
            outgoing[k, j - 1] = product(k, (p + j) % blocks).astype(jnp.bfloat16)
            sum_copy(k, j).start()
            return carry

        lax.fori_loop(1, blocks, others, 0)
        own[k] = product(k, p)

    def cot_place(owner):
        return pl.ds(pl.multiple_of(owner * lanes, lanes), lanes)

    def cot_copy(j):
        return remote(
            cot_ref.at[:, :, cot_place(peers[j])],
            cot_in.at[p],
            cot_send.at[j],
            cot_recv.at[p],
            peers[j],
            shard,
        )

    def cot_arrival(j):
        place = cot_in.at[froms[j]]
        return remote(place, place, cot_send.at[j], cot_recv.at[froms[j]], froms[j], shard)

    cot_keep = pltpu.make_async_copy(
        cot_ref.at[:, :, cot_place(p)], cot_in.at[p], cot_local.at[0]
    )
    panel_copies = [
        pltpu.make_async_copy(
            ref.at[pl.ds(c * width, width), pl.ds(r * lanes, lanes)],
            panels.at[r, c, :, pl.ds(branch * lanes, lanes)],
            panel_sem.at[branch, r, c],
        )
        for branch, ref in ((0, key_ref), (1, value_ref))
        for r in range(blocks)
        for c in range(2)
    ]

    def run(prepare):
        hop(0, 0)
        for j in range(1, blocks):
            cot_copy(j).start()
        cot_keep.start()
        for copy in panel_copies:
            copy.start()
        prepare()
        hop(0, 1)
        hop(0, 2)
        hop(1, 0)
        hop(0, 3)
        for k in range(1, chunks):
            hop(k, 1)
            hop(k, 2)
            if k + 1 < chunks:
                hop(k + 1, 0)
            share(k - 1)
            hop(k, 3)
            complete(k - 1)
            if k == 1:
                for copy in panel_copies:
                    copy.wait()
            project(k - 1)
        share(chunks - 1)
        cot_keep.wait()
        for j in range(1, blocks):
            cot_arrival(j).wait_recv()
        complete(chunks - 1)
        project(chunks - 1)

    def collect(w):
        for k in (2 * w, 2 * w + 1):
            for j in range(1, blocks):
                sum_copy(k, j).wait_recv()
            total = own[k]
            for j in range(1, blocks):
                total += incoming[k, j - 1].astype(jnp.float32)
            total = total.astype(jnp.bfloat16).reshape(blocks, rows, 2 * lanes)
            place = pl.ds(k % 2 * rows, rows)
            keys_ref[k // 2, :, place, :] = total[:, :, 0:lanes]
            values_ref[k // 2, :, place, :] = total[:, :, lanes : 2 * lanes]

    def drain():
        for k in range(chunks):
            for j in range(1, blocks):
                sum_copy(k, j).wait_send()
            for j in range(blocks):
                core_copy(features.at[core, k, froms[j]], froms[j], k).wait_send()
            for h in range(blocks):
                for way, layer, valid, onward in steps(h):
                    if h > 0:
                        onward = jnp.logical_and(valid, onward)

                    @pl.when(onward)
                    def _():
                        line_copy(h, layer, k, way).wait_send()

                    if h > 0 or way == 0:
                        sent = layer != p
                        if h > 0:
                            sent = jnp.logical_and(valid, sent)

                        @pl.when(sent)
                        def _():
                            plane_copy(h, layer, k).wait_send()

        for j in range(1, blocks):
            cot_copy(j).wait_send()

    return run, collect, drain


def gradients(
    act_ref,
    mixed_ref,
    small_ref,
    mixed_out,
    key_out,
    value_out,
    small_out,
    features,
    turned,
    got,
    mixed_in,
    small_in,
    act_send,
    act_recv,
    mixed_send,
    mixed_recv,
    small_send,
    small_recv,
):
    seqs, blocks, count, both = act_ref.shape
    lanes = both // 2
    width = features.shape[-1]
    p, shard = lax.axis_index("dp"), lax.axis_index("shard")
    x, y = p % 2, p // 2
    beside, above, across = y * 2 + 1 - x, (1 - y) * 2 + x, (1 - y) * 2 + 1 - x
    owners = (p, beside, above, across)

    span = blocks // 2

    def half_of(ref, w, half):
        return ref.at[w, pl.ds(half * span, span)]

    def send_own(slot, w, half):
        return remote(
            half_of(act_ref, w, half),
            half_of(got.at[slot - 1], w, half),
            act_send.at[slot - 1, w, half],
            act_recv.at[slot - 1, w, half],
            owners[slot],
            shard,
        )

    def pass_on(w, half):
        return remote(
            half_of(got.at[half], w, half),
            half_of(got.at[2], w, half),
            act_send.at[2, w, half],
            act_recv.at[2, w, half],
            owners[2 - half],
            shard,
        )

    def arrived(slot, w, half):
        place = half_of(got.at[slot - 1], w, half)
        return remote(
            place,
            place,
            act_send.at[slot - 1, w, half],
            act_recv.at[slot - 1, w, half],
            owners[slot],
            shard,
        )

    def mixed_copy(k):
        return remote(
            mixed_ref.at[owners[k]],
            mixed_in.at[k - 1],
            mixed_send.at[k - 1],
            mixed_recv.at[k - 1],
            owners[k],
            shard,
        )

    def small_copy(k):
        return remote(
            small_ref,
            small_in.at[k - 1],
            small_send.at[k - 1],
            small_recv.at[k - 1],
            owners[k],
            shard,
        )

    def turn(c):
        def tile(i, carry):
            k, block = i // blocks, i % blocks
            rows = count // 2
            begin = ((k // 2 * blocks + block) * 2 + k % 2) * rows
            columns = pl.ds(pl.multiple_of(begin, rows), rows)
            turned[c, :, columns] = features[c, k, block].T
            return carry

        lax.fori_loop(0, 2 * seqs * blocks, tile, 0)

    def grads(ref, owner):
        place = pl.ds(pl.multiple_of(owner * lanes, lanes), lanes)
        tall = width // 2

        def tile(i, carry):
            c, half = i // 2, i % 2
            rows = pl.ds(pl.multiple_of(half * tall, tall), tall)
            total = jnp.dot(
                turned[c, rows, :],
                ref[...].reshape(seqs * blocks * count, both),
                preferred_element_type=jnp.float32,
            ).astype(jnp.bfloat16)
            out = pl.ds(pl.multiple_of(i * tall, tall), tall)
            key_out[out, place] = total[:, :lanes]
            value_out[out, place] = total[:, lanes:]
            return carry

        lax.fori_loop(0, 4, tile, 0)

    def send(w):
        for slot, half in ((1, 0), (2, 1), (1, 1), (2, 0)):
            send_own(slot, w, half).start()

    def forward(w):
        for half in range(2):
            arrived(1 + half, w, half).wait_recv()
            pass_on(w, half).start()

    def spread():
        for k in range(1, blocks):
            mixed_copy(k).start()
            small_copy(k).start()

    def run():
        forward(0)
        turn(0)
        forward(1)
        turn(1)
        grads(act_ref, p)
        for slot, owner in ((1, beside), (2, above)):
            for w in range(seqs):
                arrived(slot, w, 2 - slot).wait_recv()
            grads(got.at[slot - 1], owner)
        small_out[p] = small_ref[...]
        for k in range(1, blocks):
            small_copy(k).wait_recv()
            small_out[owners[k]] = small_in[k - 1]
        mixed_out[:, :, pl.ds(pl.multiple_of(p * lanes, lanes), lanes)] = mixed_ref[p]
        for k in range(1, blocks):
            mixed_copy(k).wait_recv()
            place = pl.ds(pl.multiple_of(owners[k] * lanes, lanes), lanes)
            mixed_out[:, :, place] = mixed_in[k - 1]
        for w in range(seqs):
            for half in range(2):
                arrived(3, w, half).wait_recv()
        grads(got.at[2], across)
        for w in range(seqs):
            for half in range(2):
                send_own(1, w, half).wait_send()
                send_own(2, w, half).wait_send()
                pass_on(w, half).wait_send()
        for k in range(1, blocks):
            mixed_copy(k).wait_send()
            small_copy(k).wait_send()

    return send, forward, spread, run


def operator_kernel(taps, group, *refs):
    (x_ref, key_ref, value_ref, cot_ref, lengths_ref, short_ref, medium_ref, reversed_ref) = refs[:8]
    outs, keys_ref, values_ref = refs[8:12], refs[12], refs[13]
    act_ref, mixed_ref, small_ref = refs[14:17]
    front_refs, filter_refs, back_refs = refs[17:37], refs[37:46], refs[46:]
    features, cot_in = front_refs[1], front_refs[6]
    project, collect, drain = front(
        x_ref, key_ref, value_ref, cot_ref, keys_ref, values_ref, *front_refs
    )
    setup, window, finish = filters(
        taps,
        group,
        lengths_ref,
        keys_ref,
        values_ref,
        cot_in,
        short_ref,
        medium_ref,
        reversed_ref,
        mixed_ref,
        act_ref,
        small_ref,
        *filter_refs,
    )
    send, forward, spread, run = gradients(
        act_ref, mixed_ref, small_ref, *outs, features, *back_refs
    )
    project(setup)
    for w in range(keys_ref.shape[0]):
        collect(w)
        window(w)
        send(w)
    finish()
    spread()
    run()
    drain()


def operator(inputs, key_panel, value_panel, cotangent, lengths, short_filters, medium_filters, blocks):
    seqs, count, width = inputs.shape
    channels = key_panel.shape[1]
    lanes = channels // blocks
    groups, medium = medium_filters.shape
    taps = short_filters.shape[-1]
    length = blocks * count
    short = jnp.pad(short_filters.transpose(0, 2, 1), ((0, 0), (0, 8 - taps), (0, 0)))
    ahead = jnp.pad(medium_filters, ((0, 0), (0, 2 * BLOCK - medium)))
    behind = jnp.pad(medium_filters[:, ::-1], ((0, 0), (BLOCK + 1 - medium, BLOCK - 1)))
    pieces = 2 * seqs
    tall = blocks * count // 2
    vmem = pl.BlockSpec(memory_space=pltpu.VMEM)
    hbm = pl.BlockSpec(memory_space=pl.ANY)
    dma = pltpu.SemaphoreType.DMA
    small_shape = (16 + 2 * groups, lanes)
    act_shape = (seqs, blocks, count, 2 * lanes)
    panel = jax.ShapeDtypeStruct((2 * width, channels), jnp.bfloat16)
    return pl.pallas_call(
        functools.partial(operator_kernel, taps, lanes // groups),
        out_shape=(
            jax.ShapeDtypeStruct((seqs, count, channels), jnp.bfloat16),
            panel,
            panel,
            jax.ShapeDtypeStruct((blocks,) + small_shape, jnp.float32),
        ),
        in_specs=[hbm] * 4 + [pl.BlockSpec(memory_space=pltpu.SMEM)] + [vmem] * 3,
        out_specs=[vmem] * 4,
        scratch_shapes=[
            pltpu.VMEM((seqs, blocks, count, lanes), jnp.bfloat16),
            pltpu.VMEM((seqs, blocks, count, lanes), jnp.bfloat16),
            pltpu.VMEM(act_shape, jnp.bfloat16),
            pltpu.VMEM((blocks, seqs, count, lanes), jnp.bfloat16),
            pltpu.VMEM(small_shape, jnp.float32),
            pltpu.VMEM((blocks, pieces, count // 2, width), jnp.bfloat16),
            pltpu.VMEM((2, pieces, blocks, count // 2, width), jnp.bfloat16),
            pltpu.VMEM((blocks, 2, width, 2 * lanes), jnp.bfloat16),
            pltpu.VMEM((pieces, tall, 2 * lanes), jnp.float32),
            pltpu.VMEM((pieces, blocks - 1, tall, 2 * lanes), jnp.bfloat16),
            pltpu.VMEM((pieces, blocks - 1, tall, 2 * lanes), jnp.bfloat16),
            pltpu.VMEM((blocks, seqs, count, lanes), jnp.bfloat16),
            dma((2, blocks, pieces)),
            dma((blocks, pieces)),
            dma((blocks, pieces)),
            dma((blocks, pieces)),
            dma((blocks, pieces)),
            dma((blocks, pieces)),
            dma((pieces, blocks - 1)),
            dma((pieces, blocks - 1)),
            dma((blocks,)),
            dma((blocks,)),
        ]
        + [dma((pieces,)), dma((2, blocks, 2)), dma((1,))]
        + [
            pltpu.VMEM((2, seqs, length + 8, lanes), jnp.float32),
            pltpu.VMEM((2, seqs, length, lanes), jnp.float32),
            pltpu.VMEM((2, seqs, length + 8, lanes), jnp.float32),
            pltpu.VMEM((length + BLOCK, seqs * lanes), jnp.bfloat16),
            pltpu.VMEM((length + BLOCK, seqs * lanes), jnp.bfloat16),
            pltpu.VMEM((groups * BLOCK, 2 * BLOCK), jnp.bfloat16),
            pltpu.VMEM((groups * BLOCK, 2 * BLOCK), jnp.bfloat16),
            pltpu.VMEM((groups * BLOCK, 2 * BLOCK), jnp.float32),
            pltpu.VMEM((2, taps, 8, lanes), jnp.float32),
            pltpu.VMEM((2, width, seqs * blocks * count), jnp.bfloat16),
            pltpu.VMEM((3,) + act_shape, jnp.bfloat16),
            pltpu.VMEM((blocks - 1, seqs, count, lanes), jnp.bfloat16),
            pltpu.VMEM((blocks - 1,) + small_shape, jnp.float32),
            dma((3, seqs, 2)),
            dma((3, seqs, 2)),
            dma((blocks - 1,)),
            dma((blocks - 1,)),
            dma((blocks - 1,)),
            dma((blocks - 1,)),
        ],
        compiler_params=pltpu.CompilerParams(
            collective_id=0, has_side_effects=True, vmem_limit_bytes=62 * 1024 * 1024
        ),
        cost_estimate=pl.CostEstimate(
            flops=8 * blocks * seqs * count * 2 * width * channels,
            bytes_accessed=8 * blocks * seqs * count * width,
            transcendentals=0,
        ),
    )(inputs, key_panel, value_panel, cotangent, lengths, short, ahead, behind)


def by_channels(inputs, key_panel, value_panel, short_filters, medium_filters, lengths, cotangent):
    blocks = lax.axis_size("dp")
    channels = key_panel.shape[1]
    lanes = channels // blocks
    groups = medium_filters.shape[0] // blocks
    mine = lax.axis_index("dp")
    short = lax.dynamic_slice_in_dim(short_filters, mine * lanes, lanes, 1)
    medium = lax.dynamic_slice_in_dim(medium_filters, mine * groups, groups, 0)
    mixed, key_grad, value_grad, small = operator(
        inputs, key_panel, value_panel, cotangent, lengths, short, medium, blocks
    )
    taps, medium_taps = short_filters.shape[-1], medium_filters.shape[-1]
    short_grad = small[:, :16].reshape(blocks, 2, 8, lanes)[:, :, :taps]
    short_grad = short_grad.transpose(1, 0, 3, 2).reshape(2, channels, taps)
    sums = small[:, 16:].reshape(blocks, 2, groups, BLOCK).transpose(0, 2, 1, 3)
    sums = sums.reshape(blocks * groups, 2 * BLOCK)
    medium_grad = sums[:, BLOCK - medium_taps + 1 : BLOCK + 1][:, ::-1]
    return (mixed, key_grad, value_grad, short_grad, medium_grad)


def shards(inputs, key_panel, value_panel, short_filters, medium_filters, lengths, cotangent):
    blocks, shard = lax.axis_size("dp"), lax.axis_size("shard")
    channels = key_panel.shape[1]
    whole = channels == blocks * BLOCK and inputs.shape[1] % (2 * BLOCK) == 0
    plan = by_channels if whole and blocks == 4 and shard == 2 * blocks else by_positions
    return plan(
        inputs, key_panel, value_panel, short_filters, medium_filters, lengths, cotangent
    )


def solution(mesh):
    return jax.shard_map(
        shards,
        mesh=mesh,
        in_specs=(
            P(None, "dp", "shard"),
            P("dp", "shard"),
            P("dp", "shard"),
            P(None, "shard", None),
            P("shard", None),
            P(),
            P(None, "dp", "shard"),
        ),
        out_specs=(
            P(None, "dp", "shard"),
            P("dp", "shard"),
            P("dp", "shard"),
            P(None, "shard", None),
            P("shard", None),
        ),
        check_vma=False,
    )
```

time: 193 us -> 178 us (0.922)
  Pallas kernels: 182 us -> 165 us
    pallas_call x3 -> x1, Pallas kernels: 182 us -> 165 us  [operator(): pl.pallas_call(functools.partial(operator_kernel, taps, lanes // groups),...]
    unnamed x16 -> x8, local copies, waits for them, and re-layouts: 8.33 us -> 6.4 us
where the time goes in v5:
time: 178 us; the launch traced here: 177 us
  Pallas kernels  165 us (93%)
  local copies, waits for them, and re-layouts  11.2 us (6%)
    pallas_call x1, Pallas kernels, operator(): pl.pallas_call(functools.partial(operator_kernel, taps, lanes // groups),...  165 us
    unnamed x8, local copies, waits for them, and re-layouts  6.4 us

profile of v5, /device:TPU:0, one launch (start us, length us, event | category | flops | bytes accessed | tf_op | source)
XLA Modules:
  0.0 177.0 jit_solution(7507703253604255353)
XLA Ops:
  0.6 0.0 copy-start
  0.7 0.7 constant_dynamic-slice_fusion
  1.3 0.1 rev.6
  1.4 0.6 pad.13.refs_6_
  2.0 0.7 pad.14.refs_7_
  2.7 0.0 copy-done
  2.7 0.6 pad.12.refs_5_
  3.3 165.1 %shard_map.110 = (bf16[2,256,512]{2,1,0:T(8,128)(2,1)}, bf16[2048,512]{1,0:T(8,128)(2,1)}, bf16[2048,512]{1,0:T(8,128)(2,1)}, f32[4,32,128]{2,1,0:T(8,128)}) custom-call(bf16[2,256,1024]{2,1,0:T(8,128)(2,1)} %refs_0_.1, bf16[2048,512]{1,0:T(8,128)(2,1)} %refs_1_.1, bf16[2048,512]{1,0:T(8,128)(2,1)} %refs_2_.1, bf16[2,256,512]{2,1,0:T(8,128)(2,1)} %refs_3_.1, ...), custom_call_target="tpu_custom_call" | custom-call | flops 17179869184 | bytes 16777216 | tf_op jit(solution)/shard_map/pallas_call | solution.py:811
  168.5 0.8 slice_bitcast_fusion.1
  169.2 0.1 slice.17
  169.3 0.7 rev.7
  170.0 0.6 reshape.23
  170.7 1.9 %copy.20 = bf16[2,256,512]{2,1,0:T(8,128)(2,1)} copy(bf16[2,256,512]{2,1,0:T(8,128)(2,1)} %get-tuple-element.20) | data formatting | bytes 1048576
  172.5 0.0 copy-start.1
  172.5 3.2 %copy.21 = bf16[2048,512]{1,0:T(8,128)(2,1)} copy(bf16[2048,512]{1,0:T(8,128)(2,1)} %get-tuple-element.21) | data formatting | bytes 4194304
  175.7 0.0 copy-done.1
  175.7 1.3 copy.22
  (4 shorter events, 0.0 us)
Async XLA Ops:
  0.6 2.1 %copy-start = (f32[2,512,7]{1,0,2:T(2,128)S(1)}, f32[2,512,7]{1,0,2:T(2,128)}, u32[]{:S(2)}) copy-start(f32[2,512,7]{1,0,2:T(2,128)} %param.10) | copy-start | bytes 86020
  172.5 3.2 %copy-start.1 = (bf16[2048,512]{1,0:T(8,128)(2,1)S(1)}, bf16[2048,512]{1,0:T(8,128)(2,1)}, u32[]{:S(2)}) copy-start(bf16[2048,512]{1,0:T(8,128)(2,1)} %get-tuple-element.22) | copy-start | bytes 6291460

commit v6 on v5

--- a/solution.py
+++ b/solution.py
@@ -8,6 +8,7 @@
 from jax.sharding import PartitionSpec as P
 
 BLOCK = 128
+PARTS = 4
 
 
 def shifted(value, axis, steps):
@@ -331,8 +332,8 @@
 ):
     seqs, count, width = x_ref.shape
     blocks, lanes = cot_in.shape[0], cot_in.shape[-1]
-    rows = count // 2
-    chunks = 2 * seqs
+    rows = count // PARTS
+    chunks = PARTS * seqs
     p, shard = lax.axis_index("dp"), lax.axis_index("shard")
     z, core = shard // 2, shard % 2
     sibling = z * 2 + (1 - core)
@@ -358,7 +359,7 @@
     pl.semaphore_wait(barrier, blocks + 2)
 
     def block_of(k):
-        return x_ref.at[k // 2, pl.ds(k % 2 * rows, rows)]
+        return x_ref.at[k // PARTS, pl.ds(k % PARTS * rows, rows)]
 
     def held(h, layer, k):
         return block_of(k) if h == 0 else line.at[layer, k]
@@ -548,16 +549,16 @@
         project(chunks - 1)
 
     def collect(w):
-        for k in (2 * w, 2 * w + 1):
+        for k in range(PARTS * w, PARTS * (w + 1)):
             for j in range(1, blocks):
                 sum_copy(k, j).wait_recv()
             total = own[k]
             for j in range(1, blocks):
                 total += incoming[k, j - 1].astype(jnp.float32)
             total = total.astype(jnp.bfloat16).reshape(blocks, rows, 2 * lanes)
-            place = pl.ds(k % 2 * rows, rows)
-            keys_ref[k // 2, :, place, :] = total[:, :, 0:lanes]
-            values_ref[k // 2, :, place, :] = total[:, :, lanes : 2 * lanes]
+            place = pl.ds(k % PARTS * rows, rows)
+            keys_ref[k // PARTS, :, place, :] = total[:, :, 0:lanes]
+            values_ref[k // PARTS, :, place, :] = total[:, :, lanes : 2 * lanes]
 
     def drain():
         for k in range(chunks):
@@ -679,7 +680,8 @@
             rows = count // 2
             begin = ((k // 2 * blocks + block) * 2 + k % 2) * rows
             columns = pl.ds(pl.multiple_of(begin, rows), rows)
-            turned[c, :, columns] = features[c, k, block].T
+            pair = features[c, pl.ds(k * (PARTS // 2), PARTS // 2), block]
+            turned[c, :, columns] = pair.reshape(rows, width).T
             return carry
 
         lax.fori_loop(0, 2 * seqs * blocks, tile, 0)
@@ -800,8 +802,8 @@
     short = jnp.pad(short_filters.transpose(0, 2, 1), ((0, 0), (0, 8 - taps), (0, 0)))
     ahead = jnp.pad(medium_filters, ((0, 0), (0, 2 * BLOCK - medium)))
     behind = jnp.pad(medium_filters[:, ::-1], ((0, 0), (BLOCK + 1 - medium, BLOCK - 1)))
-    pieces = 2 * seqs
-    tall = blocks * count // 2
+    pieces = PARTS * seqs
+    tall = blocks * count // PARTS
     vmem = pl.BlockSpec(memory_space=pltpu.VMEM)
     hbm = pl.BlockSpec(memory_space=pl.ANY)
     dma = pltpu.SemaphoreType.DMA
@@ -824,8 +826,8 @@
             pltpu.VMEM(act_shape, jnp.bfloat16),
             pltpu.VMEM((blocks, seqs, count, lanes), jnp.bfloat16),
             pltpu.VMEM(small_shape, jnp.float32),
-            pltpu.VMEM((blocks, pieces, count // 2, width), jnp.bfloat16),
-            pltpu.VMEM((2, pieces, blocks, count // 2, width), jnp.bfloat16),
+            pltpu.VMEM((blocks, pieces, count // PARTS, width), jnp.bfloat16),
+            pltpu.VMEM((2, pieces, blocks, count // PARTS, width), jnp.bfloat16),
             pltpu.VMEM((blocks, 2, width, 2 * lanes), jnp.bfloat16),
             pltpu.VMEM((pieces, tall, 2 * lanes), jnp.float32),
             pltpu.VMEM((pieces, blocks - 1, tall, 2 * lanes), jnp.bfloat16),

time: 178 us -> 174 us (0.978)
  Pallas kernels: 165 us -> 161 us
    pallas_call x1, Pallas kernels: 165 us -> 161 us  [operator(): pl.pallas_call(functools.partial(operator_kernel, taps, lanes // groups),...]
where the time goes in v6:
time: 174 us; the launch traced here: 172 us
  Pallas kernels  161 us (93%)
  local copies, waits for them, and re-layouts  11.2 us (6%)
    pallas_call x1, Pallas kernels, operator(): pl.pallas_call(functools.partial(operator_kernel, taps, lanes // groups),...  161 us
    unnamed x8, local copies, waits for them, and re-layouts  6.4 us

profile of v6, /device:TPU:0, one launch (start us, length us, event | category | flops | bytes accessed | tf_op | source)
XLA Modules:
  0.0 172.5 jit_solution(14684203894099152814)
XLA Ops:
  0.6 0.0 copy-start
  0.7 0.7 constant_dynamic-slice_fusion
  1.3 0.1 rev.6
  1.4 0.6 pad.13.refs_6_
  2.0 0.7 pad.14.refs_7_
  2.7 0.0 copy-done
  2.7 0.6 pad.12.refs_5_
  3.3 160.6 %shard_map.110 = (bf16[2,256,512]{2,1,0:T(8,128)(2,1)}, bf16[2048,512]{1,0:T(8,128)(2,1)}, bf16[2048,512]{1,0:T(8,128)(2,1)}, f32[4,32,128]{2,1,0:T(8,128)}) custom-call(bf16[2,256,1024]{2,1,0:T(8,128)(2,1)} %refs_0_.1, bf16[2048,512]{1,0:T(8,128)(2,1)} %refs_1_.1, bf16[2048,512]{1,0:T(8,128)(2,1)} %refs_2_.1, bf16[2,256,512]{2,1,0:T(8,128)(2,1)} %refs_3_.1, ...), custom_call_target="tpu_custom_call" | custom-call | flops 17179869184 | bytes 16777216 | tf_op jit(solution)/shard_map/pallas_call | solution.py:813
  163.9 0.8 slice_bitcast_fusion.1
  164.7 0.1 slice.17
  164.7 0.7 rev.7
  165.4 0.6 reshape.23
  166.1 1.9 %copy.20 = bf16[2,256,512]{2,1,0:T(8,128)(2,1)} copy(bf16[2,256,512]{2,1,0:T(8,128)(2,1)} %get-tuple-element.20) | data formatting | bytes 1048576
  168.0 0.0 copy-start.1
  168.0 3.2 %copy.21 = bf16[2048,512]{1,0:T(8,128)(2,1)} copy(bf16[2048,512]{1,0:T(8,128)(2,1)} %get-tuple-element.21) | data formatting | bytes 4194304
  171.1 0.0 copy-done.1
  171.1 1.3 copy.22
  (4 shorter events, 0.0 us)
Async XLA Ops:
  0.6 2.1 %copy-start = (f32[2,512,7]{1,0,2:T(2,128)S(1)}, f32[2,512,7]{1,0,2:T(2,128)}, u32[]{:S(2)}) copy-start(f32[2,512,7]{1,0,2:T(2,128)} %param.10) | copy-start | bytes 86020
  168.0 3.2 %copy-start.1 = (bf16[2048,512]{1,0:T(8,128)(2,1)S(1)}, bf16[2048,512]{1,0:T(8,128)(2,1)}, u32[]{:S(2)}) copy-start(bf16[2048,512]{1,0:T(8,128)(2,1)} %get-tuple-element.22) | copy-start | bytes 6291460
